TPU v7x, 128 devices: a whole 4x4x4 slice. The times are simulated.
128 devices in a mesh: vocab: 16 (over y, z), feat: 8 (over x, core).
Axes of the slice: x: 4, y: 4, z: 4, core: 2. Of those that a mesh axis runs over, the one named last changes fastest.
Arguments:
- hidden: bfloat16 [2048, 4096], P('feat'), may hold values from -64 to 64
- out_head: bfloat16 [131072, 4096], P(('vocab', 'feat')), may hold values from -0.28125 to 0.28125
- out_proj: bfloat16 [131072, 128], P(('vocab', 'feat')), may hold values from -5 to 5
- in_proj: bfloat16 [4096, 128], replicated, may hold values from -0.09375 to 0.09375
- targets: int32 [2048], replicated, may hold values from 0 to 131071
- seq_ids: int32 [2048], replicated, may hold values from 0 to 15, never falling along the last dimension, each value on 1 to 256 neighbouring positions
- grad_store: bfloat16 [32768, 16384], P('vocab', 'feat'), may hold values from -0.01953125 to 0.01953125
Outputs:
- influence: float32 [32768, 16], P(('vocab', 'feat'))
All inputs are finite; a program needn't handle non-finite values.
Results may differ from a plain program's by a relative error of at most 0.003.
Values may be sent and summed in bfloat16 or wider, within the bound.
No kernel may reach another device: no remote copies, remote signals or barrier semaphores. Data moves between devices by JAX's collectives and lax.ppermute only.
A program may use at most 128 MiB of HBM per device.

v0:
```python
import jax
import jax.numpy as jnp
from jax import lax
from jax.sharding import Mesh
from jax.sharding import PartitionSpec as P

SEQS = 16
FEAT = ("feat_0", "feat_1")
VOCAB_FEAT = ("vocab_0", "vocab_1", "feat_0", "feat_1")
VOCAB = ("vocab_0", "vocab_1")


def all_in_one(value, axis):
    leaves = jax.tree.leaves(value)
    sequence = sorted(range(len(leaves)), key=lambda k: -leaves[k].size)
    width = (1, *leaves[sequence[0]].shape)[-1]
    lines = [
        jnp.pad(leaves[k].reshape(-1), (0, -leaves[k].size % width)).reshape(-1, width)
        for k in sequence
    ]
    both, at, found = (lax.all_gather(jnp.concatenate(lines), axis), 0, {})
    for k, line in zip(sequence, lines):
        piece = both[:, at : at + len(line)].reshape(len(both), -1)
        found[k] = piece[:, : leaves[k].size].reshape(-1, *leaves[k].shape)
        at += len(line)
    numbers = iter(range(len(leaves)))
    return jax.tree.map(lambda _: found[next(numbers)], value)


def merged_by_axis(value, axes, combine):
    for axis in axes:
        pieces = all_in_one(value, axis)
        value = jax.tree.map(lambda part: part[0], pieces)
        for k in range(1, lax.axis_size(axis)):
            value = combine(value, jax.tree.map(lambda part: part[k], pieces))
    return value


def in_blocks(value, dim, length):
    shape = value.shape
    tiles = value.reshape(*shape[:dim], length, shape[dim] // length, *shape[dim + 1 :])
    return jnp.moveaxis(tiles, dim, 0)


def summed_on_arrival(value, axis, dim):
    length = lax.axis_size(axis)
    tiles = lax.all_to_all(in_blocks(value, dim, length), axis, 0, 0, tiled=True)
    return jnp.sum(tiles, axis=0)


def copy_for_each(value, axis):
    copies = jnp.broadcast_to(value, (lax.axis_size(axis), *value.shape))
    return lax.all_to_all(copies, axis, split_axis=0, concat_axis=0, tiled=True)


def over_copies(value, axis):
    everything = copy_for_each(value, axis)
    return jnp.sum(everything, axis=0)


def combine_stats(first, second):
    merged_max = jnp.maximum(first[0], second[0])
    merged_sum = first[1] * jnp.exp(first[0] - merged_max) + second[1] * jnp.exp(
        second[0] - merged_max
    )
    return (merged_max, merged_sum)


def on_device(hidden, out_head, out_proj, in_proj, targets, seq_ids, grad_store):
    vocab_local = out_head.shape[0]
    tok_piece = lax.all_gather(hidden, FEAT, axis=0, tiled=True)
    logits = lax.dot_general(
        tok_piece, out_head, (((1,), (1,)), ((), ())), preferred_element_type=jnp.float32
    )
    projected = jnp.dot(tok_piece, in_proj, preferred_element_type=jnp.float32)
    joined = jnp.concatenate([logits, projected], axis=1)
    logits = joined[:, :vocab_local]
    in_side = joined[:, vocab_local:]
    local_max = jnp.max(logits, axis=1)
    local_sum = jnp.sum(jnp.exp(logits - local_max[:, None]), axis=1)
    global_max, global_sum = merged_by_axis((local_max, local_sum), VOCAB_FEAT, combine_stats)
    expval = jnp.exp(logits - global_max[:, None])
    offset = lax.axis_index(VOCAB_FEAT) * vocab_local
    columns = offset + lax.iota(jnp.int32, vocab_local)
    onehot = (targets[:, None] == columns[None, :]).astype(jnp.float32)
    residual = (expval / global_sum[:, None] - onehot).astype(jnp.bfloat16)
    partial_out = jnp.dot(residual, out_proj, preferred_element_type=jnp.float32)
    proj_rank = out_proj.shape[1]
    col_share = proj_rank // lax.axis_size(FEAT)
    feat_cols = summed_on_arrival(partial_out, FEAT, 1)
    out_part = over_copies(feat_cols, VOCAB)
    tok_total = out_part.shape[0]
    member = (seq_ids[:, None] == lax.iota(jnp.int32, SEQS)[None, :]).astype(jnp.float32)
    weighted = (member[:, :, None] * out_part[:, None, :]).reshape(tok_total, SEQS * col_share)
    query_grads = lax.dot_general(
        weighted,
        in_side,
        (((0,), (0,)), ((), ())),
        precision=lax.Precision.HIGHEST,
        preferred_element_type=jnp.float32,
    )
    query_grads = query_grads.reshape(SEQS, col_share * proj_rank).astype(jnp.bfloat16)
    return summed_on_arrival(
        lax.dot_general(
            grad_store, query_grads, (((1,), (1,)), ((), ())), preferred_element_type=jnp.float32
        ),
        FEAT,
        0,
    )


def solution(mesh):
    split = Mesh(mesh.devices.reshape(4, 4, 4, 2), ("vocab_0", "vocab_1", "feat_0", "feat_1"))
    return jax.shard_map(
        on_device,
        mesh=split,
        in_specs=(
            P(FEAT, None),
            P(VOCAB_FEAT, None),
            P(VOCAB_FEAT, None),
            P(),
            P(),
            P(),
            P(VOCAB, FEAT),
        ),
        out_specs=P(VOCAB_FEAT, None),
        check_vma=False,
    )
```

profile of v0, /device:TPU:1, one launch (start us, length us, event | category | flops | bytes accessed | tf_op | source)
XLA Modules:
  0.0 243.0 jit_solution(17524572532188073230)
XLA Ops:
  6.5 0.7 all-gather.10.cloned.1.call-update
  7.3 90.4 %all-gather.10.cloned.1.call-done = bf16[2048,4096]{1,0:T(8,128)(2,1)} async-done(((bf16[256,4096]{1,0:T(8,128)(2,1)}), bf16[2048,4096]{1,0:T(8,128)(2,1)}) %all-gather.10.cloned.1.call-update) | async-done | bytes 16777232 | tf_op jit(solution)/shard_map/all_gather | solution.py:71
  97.7 22.8 %fusion.42 = (f32[2048]{0:T(1024)S(1)}, f32[2048,1024]{0,1:T(8,128)S(1)}) fusion(bf16[2048,4096]{1,0:T(8,128)(2,1)} %all-gather.10.cloned.1.call-done, bf16[1024,4096]{1,0:T(8,128)(2,1)} %param.8), kind=kOutput, calls=%fused_computation.75 | convolution fusion | flops 17181964288 | bytes 33562624 | tf_op jit(solution)/shard_map/dot_general | solution.py:72
  120.5 1.2 exponential_reduce_fusion
  121.7 9.7 %all-gather.4 = f32[4,2,2048]{2,1,0:T(2,128)S(1)} all-gather(f32[1,2,2048]{2,1,0:T(2,128)S(1)} %maximum_bitcast_fusion), channel_id=2, replica_groups=mesh['vocab_0'=4,'vocab_1'=4,'feat_0'=4,'feat_1'=2] {'vocab_0'}, dimensions={0}, use_global_device_ids=true | all-gather | bytes 81920 | tf_op jit(solution)/shard_map/all_gather | solution.py:21
  131.4 0.1 fusion.21
  131.5 9.5 %all-gather.5 = f32[4,2,2048]{2,1,0:T(2,128)S(1)} all-gather(f32[1,2,2048]{2,1,0:T(2,128)S(1)} %maximum_bitcast_fusion.1), channel_id=3, replica_groups=mesh['vocab_0'=4,'vocab_1'=4,'feat_0'=4,'feat_1'=2] {'vocab_1'}, dimensions={0}, use_global_device_ids=true | all-gather | bytes 81920 | tf_op jit(solution)/shard_map/all_gather | solution.py:21
  140.9 0.1 fusion.12
  141.1 9.0 %all-gather.6 = f32[4,2,2048]{2,1,0:T(2,128)S(1)} all-gather(f32[1,2,2048]{2,1,0:T(2,128)S(1)} %maximum_bitcast_fusion.2), channel_id=4, replica_groups=mesh['vocab_0'=4,'vocab_1'=4,'feat_0'=4,'feat_1'=2] {'feat_0'}, dimensions={0}, use_global_device_ids=true | all-gather | bytes 81920 | tf_op jit(solution)/shard_map/all_gather | solution.py:21
  150.0 0.1 fusion.3
  150.2 10.1 %all-gather.7 = f32[2,2,2048]{2,1,0:T(2,128)S(1)} all-gather(f32[1,2,2048]{2,1,0:T(2,128)S(1)} %maximum_bitcast_fusion.3), channel_id=5, replica_groups=mesh['vocab_0'=4,'vocab_1'=4,'feat_0'=4,'feat_1'=2] {'feat_1'}, dimensions={0}, use_global_device_ids=true | all-gather | bytes 49152 | tf_op jit(solution)/shard_map/all_gather | solution.py:21
  160.3 2.5 %fusion = f32[2048,128]{0,1:T(8,128)S(1)} fusion(bf16[1024,128]{1,0:T(8,128)(2,1)S(1)} %copy-done.2, f32[2048,1024]{0,1:T(8,128)S(1)} %get-tuple-element.18, s32[2048]{0:T(1024)S(1)} %copy-done.3, f32[2048]{0:T(1024)S(1)} %get-tuple-element.5, f32[2048]{0:T(1024)S(1)} %get-tuple-element.6, s32[1024]{0:T(1024)S(1)} %iota_add_fusion), kind=kOutput, calls=%fused_computation.2 | convolution fusion | flops 549453824 | bytes 9728000 | tf_op jit(solution)/shard_map/dot_general | solution.py:87
  162.8 17.9 %all_to_all.15 = f32[8,2048,16]{1,2,0:T(8,128)S(1)} all-to-all(f32[8,2048,16]{1,2,0:T(8,128)S(1)} %bitcast.249), channel_id=1, replica_groups=mesh['vocab_0'=4,'vocab_1'=4,'feat_0'=4,'feat_1'=2] {'feat_0','feat_1'}, dimensions={0} | all-to-all | bytes 2097152 | tf_op jit(solution)/shard_map/all_to_all | solution.py:47
  180.7 0.1 reduce_sum.37
  180.8 1.6 broadcast_in_dim.2
  182.4 5.4 %all-to-all-start.1 = ((f32[16,2048,16]{1,2,0:T(8,128)}), f32[16,2048,16]{1,2,0:T(8,128)S(1)}, u32[]{:S(2)}, u32[]{:S(2)}) async-start(f32[16,2048,16]{1,2,0:T(8,128)} %broadcast_in_dim.2), calls=%async_computation.1 | async-start | bytes 4194304 | tf_op jit(solution)/shard_map/all_to_all | solution.py:53
  187.9 9.1 %fusion.43 = f32[2048,128]{1,0:T(8,128)} fusion(bf16[2048,4096]{1,0:T(8,128)(2,1)} %all-gather.10.cloned.1.call-done, bf16[4096,128]{1,0:T(8,128)(2,1)S(1)} %copy-done), kind=kOutput, calls=%fused_computation.76 | convolution fusion | flops 2147483648 | bytes 18874368 | tf_op jit(solution)/shard_map/dot_general | solution.py:75
  197.0 16.6 %all-to-all-done.1 = f32[16,2048,16]{1,2,0:T(8,128)S(1)} async-done(((f32[16,2048,16]{1,2,0:T(8,128)}), f32[16,2048,16]{1,2,0:T(8,128)S(1)}, u32[]{:S(2)}, u32[]{:S(2)}) %all-to-all-start.1) | async-done | bytes 2097184 | tf_op jit(solution)/shard_map/all_to_all | solution.py:53
  213.6 0.1 reduce_sum.38
  213.7 0.2 broadcast_multiply_fusion
  213.9 3.1 %convolution_convert_fusion = bf16[256,128]{1,0:T(8,128)(2,1)S(1)} fusion(f32[2048,256]{0,1:T(8,128)S(1)} %bitcast.248, f32[2048,128]{1,0:T(8,128)} %fusion.43), kind=kOutput, calls=%fused_computation.3 | convolution fusion | flops 805339136 | bytes 3211264 | tf_op jit(solution)/shard_map/dot_general | solution.py:95
  217.0 5.6 %fusion.44 = f32[16,2048]{1,0:T(8,128)S(1)} fusion(bf16[16,2048]{1,0:T(8,128)(2,1)S(1)} %convert_element_type.23, bf16[2048,2048]{1,0:T(8,128)(2,1)} %param.13), kind=kOutput, calls=%fused_computation.77 | convolution fusion | flops 134217728 | bytes 8585216 | tf_op jit(solution)/shard_map/dot_general | solution.py:104
  222.7 12.9 %all_to_all.16 = f32[8,256,16]{1,2,0:T(8,128)S(1)} all-to-all(f32[8,256,16]{1,2,0:T(8,128)S(1)} %bitcast.251), channel_id=1, replica_groups=mesh['vocab_0'=4,'vocab_1'=4,'feat_0'=4,'feat_1'=2] {'feat_0','feat_1'}, dimensions={0} | all-to-all | bytes 262144 | tf_op jit(solution)/shard_map/all_to_all | solution.py:47
  235.6 0.6 reduce_sum.39
  (19 shorter events, 0.2 us)
Async XLA Ops:
  6.5 181.3 %copy-start = (bf16[4096,128]{1,0:T(8,128)(2,1)S(1)}, bf16[4096,128]{1,0:T(8,128)(2,1)}, u32[]{:S(2)}) copy-start(bf16[4096,128]{1,0:T(8,128)(2,1)} %param.10) | copy-start | bytes 3145732
  6.5 91.1 %all-gather.10.cloned.1.call-start = ((), (), s32[]{:S(2)}) async-start(), calls=%async_computation.3 | async-start | bytes 18874368 | tf_op jit(solution)/shard_map/all_gather | solution.py:71
  120.5 39.8 %copy-start.2 = (bf16[1024,128]{1,0:T(8,128)(2,1)S(1)}, bf16[1024,128]{1,0:T(8,128)(2,1)}, u32[]{:S(2)}) copy-start(bf16[1024,128]{1,0:T(8,128)(2,1)} %param.9) | copy-start | bytes 786436
  120.5 39.8 %copy-start.3 = (s32[2048]{0:T(1024)S(1)}, s32[2048]{0:T(1024)}, u32[]{:S(2)}) copy-start(s32[2048]{0:T(1024)} %param.11) | copy-start | bytes 24580
  162.8 25.0 %copy-start.1 = (s32[2048]{0:T(1024)S(1)}, s32[2048]{0:T(1024)}, u32[]{:S(2)}) copy-start(s32[2048]{0:T(1024)} %param.12) | copy-start | bytes 24580
  182.4 31.2 %all-to-all-start.1 = ((f32[16,2048,16]{1,2,0:T(8,128)}), f32[16,2048,16]{1,2,0:T(8,128)S(1)}, u32[]{:S(2)}, u32[]{:S(2)}) async-start(f32[16,2048,16]{1,2,0:T(8,128)} %broadcast_in_dim.2), calls=%async_computation.1 | async-start | bytes 4194304 | tf_op jit(solution)/shard_map/all_to_all | solution.py:53
Sparse Core Ops, SparseCore 0:
  9.1 88.5 all-gather.9
where the time goes:
time: 243 us
  waiting for transfers between devices  108 us (44%)
  blocking collectives  69 us (28%)
  matrix products  43.1 us (18%)
  between operations  13.6 us (6%)
  starting transfers between devices  5.43 us (2%)
  other arithmetic  2.56 us (1%)
    all_gather x1, waiting for transfers between devices, on_device(): tok_piece = lax.all_gather(hidden, FEAT, axis=0, tiled=True)  90.4 us
    all_gather x4, blocking collectives, all_in_one(): both, at, found = (lax.all_gather(jnp.concatenate(lines), axis), 0, {})  38.2 us
    all_to_all x2, blocking collectives, summed_on_arrival(): lax.all_to_all(in_blocks(value, dim, length), axis, 0, 0, tiled=True)  30.8 us
    dot_general x1, matrix products, on_device(): lax.dot_general(tok_piece, out_head, (((1,), (1,)), ((), ())), preferred_...  22.8 us
    all_to_all x1, waiting for transfers between devices, copy_for_each(): return lax.all_to_all(copies, axis, split_axis=0, concat_axis=0, tiled=True)  16.6 us
    dot_general x1, matrix products, on_device(): projected = jnp.dot(tok_piece, in_proj, preferred_element_type=jnp.float32)  9.13 us
    dot_general x1, matrix products, on_device(): lax.dot_general(grad_store, query_grads, (((1,), (1,)), ((), ())), prefer...  5.65 us
    all_to_all x1, starting transfers between devices, copy_for_each(): return lax.all_to_all(copies, axis, split_axis=0, concat_axis=0, tiled=True)  5.43 us
  transfers between devices with their start and end apart: 2, of which 2 were waited for; matrix products, arithmetic and copies ran while one was open for 4% of the time, Pallas kernels for 0%

commit v1 on v0

v1 whole, which is shorter than its diff:
```python
import functools

import jax
import jax.numpy as jnp
from jax import lax
from jax.experimental import pallas as pl
from jax.experimental.pallas import tpu as pltpu
from jax.sharding import Mesh
from jax.sharding import PartitionSpec as P

SEQS = 16
ALL = ("y", "z", "x", "c")
TILE = 256
BF = jnp.bfloat16
F32 = jnp.float32


def index(y, z, x, c):
    return (((y % 4) * 4 + z % 4) * 4 + x % 4) * 2 + c


def move(value, target):
    pairs = [
        (index(y, z, x, c), index(*target(y, z, x, c)))
        for y in range(4)
        for z in range(4)
        for x in range(4)
        for c in range(2)
    ]
    return lax.ppermute(value, ALL, pairs)


def along_x(y, z, x, c):
    return (y, z, x + 1 - 2 * c, c)


def along_x_crossed(y, z, x, c):
    return (y, z, x - 1 + 2 * c, 1 - c)


def along_y(y, z, x, c):
    return (y + 1 - 2 * c, z, x, c)


def along_z(y, z, x, c):
    return (y, z + 1 - 2 * c, x, c)


def to_sibling(y, z, x, c):
    return (y, z, x, 1 - c)


def flash_kernel(sizes, tiles, *refs):
    count = len(sizes)
    pieces = refs[:count]
    own_ref, sib_ref, proj_ref, in_ref, out_ref, lse_ref, side_ref, tok, scores = refs[count:]
    step = pl.program_id(0)

    @pl.when(step == 0)
    def _():
        at = 0
        for size, piece in zip(sizes, pieces):
            tok[at : at + size, :] = piece[...]
            at += size
        side_ref[...] = jnp.dot(tok[...], in_ref[...], preferred_element_type=F32)

    dims = (((1,), (1,)), ((), ()))

    @pl.when(step < tiles // 2)
    def _():
        scores[step] = lax.dot_general(tok[...], own_ref[...], dims, preferred_element_type=F32)

    @pl.when(step >= tiles // 2)
    def _():
        scores[step] = lax.dot_general(tok[...], sib_ref[...], dims, preferred_element_type=F32)

    @pl.when(step == tiles - 1)
    def _():
        best = scores[0]
        for t in range(1, tiles):
            best = jnp.maximum(best, scores[t])
        best = jnp.max(best, axis=1, keepdims=True)
        total = None
        mixed = None
        for t in range(tiles):
            power = jnp.exp(scores[t] - best)
            total = power if t == 0 else total + power
            part = jnp.dot(
                power.astype(BF), proj_ref[t * TILE : (t + 1) * TILE, :], preferred_element_type=F32
            )
            mixed = part if t == 0 else mixed + part
        total = jnp.sum(total, axis=1, keepdims=True)
        out_ref[...] = mixed / total
        lse_ref[...] = jnp.broadcast_to(best + jnp.log(total), lse_ref.shape)


def flash(pieces, own, sib, proj, in_proj):
    sizes = tuple(p.shape[0] for p in pieces)
    n = sum(sizes)
    depth = own.shape[1]
    rows = own.shape[0]
    rank = proj.shape[1]
    half = rows // TILE
    tiles = 2 * half
    whole = lambda shape: pl.BlockSpec(shape, lambda i: (0, 0))
    return pl.pallas_call(
        functools.partial(flash_kernel, sizes, tiles),
        grid=(tiles,),
        in_specs=[whole(p.shape) for p in pieces]
        + [
            pl.BlockSpec((TILE, depth), lambda i: (jnp.minimum(i, half - 1), 0)),
            pl.BlockSpec((TILE, depth), lambda i: (jnp.maximum(i - half, 0), 0)),
            whole(proj.shape),
            whole(in_proj.shape),
        ],
        out_specs=[whole((n, rank))] * 3,
        out_shape=[jax.ShapeDtypeStruct((n, rank), F32)] * 3,
        scratch_shapes=[pltpu.VMEM((n, depth), BF), pltpu.VMEM((tiles, n, TILE), F32)],
        compiler_params=pltpu.CompilerParams(vmem_limit_bytes=48 * 1024 * 1024),
        cost_estimate=pl.CostEstimate(
            flops=2 * n * 2 * rows * depth, bytes_accessed=2 * rows * depth * 2, transcendentals=0
        ),
    )(*pieces, own, sib, proj, in_proj)


def hot_kernel(where, targets_ref, proj_ref, out_ref):
    local = out_ref.shape[1]
    rows = proj_ref.shape[1]
    half = rows // 2
    total = None
    for t in range(rows // TILE):
        first = t * TILE
        base = where[0] + first if first < half else where[1] + first - half
        ids = base + lax.broadcasted_iota(jnp.int32, (TILE, local), 0)
        hot = jnp.where(ids == targets_ref[...], 1.0, 0.0).astype(BF)
        part = jnp.dot(proj_ref[:, first : first + TILE], hot, preferred_element_type=F32)
        total = part if t == 0 else total + part
    out_ref[...] = total


def hot_rows(where, targets, proj_t):
    return pl.pallas_call(
        hot_kernel,
        in_specs=[
            pl.BlockSpec(memory_space=pltpu.SMEM),
            pl.BlockSpec(memory_space=pltpu.VMEM),
            pl.BlockSpec(memory_space=pltpu.VMEM),
        ],
        out_specs=pl.BlockSpec(memory_space=pltpu.VMEM),
        out_shape=jax.ShapeDtypeStruct((proj_t.shape[0], targets.shape[1]), F32),
        compiler_params=pltpu.CompilerParams(vmem_limit_bytes=32 * 1024 * 1024),
        cost_estimate=pl.CostEstimate(
            flops=2 * 128 * 2048 * 1024, bytes_accessed=1 << 20, transcendentals=0
        ),
    )(where, targets, proj_t)


def pack_kernel(place, *refs):
    outs, lses, sides = refs[0:3], refs[3:6], refs[6:9]
    hot_ref, send_ref, side_ref, out_nat, lse_nat = refs[9:]
    k = place[0]
    spot = [place[1], place[2], place[3], place[4]]

    def put(slot, quarter, source, start, rows, into=0):
        for h in range(rows // 32):
            group = quarter * 2 + into + h
            at = slice(start + 32 * h, start + 32 * h + 32)
            out_nat[group, spot[slot]] = outs[source][at, :]
            lse_nat[group, spot[slot]] = lses[source][at, :]
            side_ref[group, spot[slot]] = sides[source][at, :]

    ky, kz, kd = k ^ 2, k ^ 1, k ^ 3
    for q in range(4):
        put(0, q, 0, 64 * q, 64)
    for n, (slot, quarter) in enumerate(
        [(1, k), (2, k), (1, ky), (2, ky), (1, kz), (2, kz), (3, k), (1, kd)]
    ):
        put(slot, quarter, 1, 64 * n, 64)
    put(3, ky, 2, 0, 64)
    put(2, kd, 2, 64, 32)
    put(3, kz, 2, 96, 64)
    put(2, kd, 2, 160, 32, into=1)
    put(3, kd, 2, 192, 64)

    for group in range(8):
        mixed = jnp.transpose(out_nat[group].reshape(128, 128)).reshape(16, 8, 128)
        lse = jnp.transpose(lse_nat[group].reshape(128, 128))[0:8, :]
        high = lse.astype(BF).astype(F32)
        rest = lse - high
        middle = rest.astype(BF).astype(F32)
        low = rest - middle
        line = lax.broadcasted_iota(jnp.int32, (8, 128), 0)
        stats = jnp.where(
            line == 0, high, jnp.where(line == 1, middle, jnp.where(line == 2, low, 0.0))
        )
        hot = hot_ref[:, group * 128 : group * 128 + 128].reshape(16, 8, 128)
        for part in range(16):
            to = (2 * group + part % 2) * 8 + part // 2
            send_ref[to] = jnp.concatenate([mixed[part], hot[part], stats], axis=0).astype(BF)


def pack(place, results, hot):
    outs, lses, sides = zip(*results)
    return pl.pallas_call(
        pack_kernel,
        in_specs=[pl.BlockSpec(memory_space=pltpu.SMEM)]
        + [pl.BlockSpec(memory_space=pltpu.VMEM)] * 10,
        out_specs=[pl.BlockSpec(memory_space=pltpu.VMEM)] * 2,
        out_shape=[
            jax.ShapeDtypeStruct((128, 24, 128), BF),
            jax.ShapeDtypeStruct((8, 4, 32, 128), F32),
        ],
        scratch_shapes=[pltpu.VMEM((8, 4, 32, 128), F32)] * 2,
        compiler_params=pltpu.CompilerParams(vmem_limit_bytes=32 * 1024 * 1024),
    )(place, *outs, *lses, *sides, hot)


def merge_kernel(got_ref, out_ref):
    lse = (
        got_ref[:, 16:24, :].astype(F32)
    )
    lse = lse[:, 0:1, :] + lse[:, 1:2, :] + lse[:, 2:3, :]
    source = lax.broadcasted_iota(jnp.int32, (128, 1, 128), 0)
    lane = lax.broadcasted_iota(jnp.int32, (128, 1, 128), 2)
    x = lax.div(lax.rem(source, 8), 2)
    c = lax.rem(source, 2)
    other = lax.div(lane, 32) == lax.rem(x + 1, 4)
    kind = jnp.where(other, 1 - c, c)
    halves = []
    for which in range(2):
        mine = kind == which
        best = jnp.max(jnp.where(mine, lse, -3.0e38), axis=0, keepdims=True)
        weight = jnp.where(mine, jnp.exp(jnp.minimum(lse - best, 0.0)), 0.0)
        total = jnp.sum(weight, axis=0)
        mixed = jnp.sum(weight * got_ref[:, 0:8, :].astype(F32), axis=0)
        hot = jnp.sum(jnp.where(mine, got_ref[:, 8:16, :].astype(F32), 0.0), axis=0)
        halves.append(mixed / total - hot)
    both = jnp.concatenate(halves, axis=1)
    for copy in range(16):
        out_ref[copy] = both


def merge(got):
    return pl.pallas_call(
        merge_kernel,
        in_specs=[pl.BlockSpec(memory_space=pltpu.VMEM)],
        out_specs=pl.BlockSpec(memory_space=pltpu.VMEM),
        out_shape=jax.ShapeDtypeStruct((16, 8, 256), F32),
        compiler_params=pltpu.CompilerParams(vmem_limit_bytes=32 * 1024 * 1024),
    )(got)


def score_kernel(flags, out_ref, own_ref, sib_ref, seq_ref, store_ref, result_ref, grads):
    @pl.when(pl.program_id(0) == 0)
    def _():
        total = jnp.zeros((256, 128), F32)
        for group in range(8):
            out = jnp.concatenate([out_ref[2 * group], out_ref[2 * group + 1]], axis=0)
            ids = seq_ref[group : group + 1, :]
            member = lax.broadcasted_iota(jnp.int32, (16, 256), 0) == ids
            spread = jnp.where(member[None, :, :], out[:, None, :], 0.0).reshape(256, 256)
            first, second = [], []
            for spot in range(4):
                own, sib = own_ref[group, spot], sib_ref[group, spot]
                keep = flags[spot] == 0
                first.append(jnp.where(keep, own, sib))
                second.append(jnp.where(keep, sib, own))
            side = jnp.concatenate(first + second, axis=0)
            spread_high = spread.astype(BF)
            spread_low = (spread - spread_high.astype(F32)).astype(BF)
            side_high = side.astype(BF)
            side_low = (side - side_high.astype(F32)).astype(BF)
            for a, b in (
                (spread_high, side_high),
                (spread_high, side_low),
                (spread_low, side_high),
            ):
                total += jnp.dot(a, b, preferred_element_type=F32)
        for i in range(16):
            grads[:, i * 128 : (i + 1) * 128] = total[i * 16 : (i + 1) * 16, :].astype(BF)

    result_ref[0] = lax.dot_general(
        grads[...], store_ref[...], (((1,), (1,)), ((), ())), preferred_element_type=F32
    )


def score(flags, out, own, sib, seq, store):
    fixed = lambda shape: pl.BlockSpec(shape, lambda i: (0,) * len(shape))
    return pl.pallas_call(
        score_kernel,
        grid=(8,),
        in_specs=[
            pl.BlockSpec(memory_space=pltpu.SMEM),
            fixed(out.shape),
            fixed(own.shape),
            fixed(sib.shape),
            fixed(seq.shape),
            pl.BlockSpec((store.shape[0] // 8, store.shape[1]), lambda i: (i, 0)),
        ],
        out_specs=pl.BlockSpec((1, SEQS, 256), lambda i: (i, 0, 0)),
        out_shape=jax.ShapeDtypeStruct((8, SEQS, 256), F32),
        scratch_shapes=[pltpu.VMEM((SEQS, store.shape[1]), BF)],
        compiler_params=pltpu.CompilerParams(vmem_limit_bytes=32 * 1024 * 1024),
    )(flags, out, own, sib, seq, store)


def finish_kernel(got_ref, out_ref):
    total = got_ref[0]
    for source in range(1, 8):
        total = total + got_ref[source]
    out_ref[...] = jnp.transpose(total)


def finish(got):
    return pl.pallas_call(
        finish_kernel,
        in_specs=[pl.BlockSpec(memory_space=pltpu.VMEM)],
        out_specs=pl.BlockSpec(memory_space=pltpu.VMEM),
        out_shape=jax.ShapeDtypeStruct((256, SEQS), F32),
    )(got)


def by_place(per_token):
    table = per_token.reshape(4, 2, 256)
    return jnp.stack([table[:, 0], jnp.roll(table[:, 1], 2, axis=0)])


def on_device(hidden, out_head, out_proj, in_proj, targets, seq_ids, grad_store):
    y, z, x, c = (lax.axis_index(name) for name in ALL)
    k = 2 * (y % 2) + z % 2
    sign = 1 - 2 * c
    rows = out_head.shape[0]

    mine = lax.dynamic_slice_in_dim(hidden, k * 64, 64, 0)
    mine_d = lax.dynamic_slice_in_dim(hidden, (3 - k) * 64, 64, 0)

    near_a = move(mine, along_x)
    near_b = move(mine, along_x_crossed)
    head_sib = move(out_head, to_sibling)
    proj_sib = move(out_proj, to_sibling)
    mine_d, near_a = lax.optimization_barrier((mine_d, near_a))
    far_k = move(near_a, along_x)
    near_a_y = move(near_a, along_y)
    near_a_z = move(near_a, along_z)
    near_a_d = move(mine_d, along_x)
    near_b_y = move(near_b, along_y)
    near_b_z = move(near_b, along_z)
    last_y = move(jnp.concatenate([far_k, near_b_z[:32]], axis=0), along_y)
    last_z = move(jnp.concatenate([far_k, near_b_y[32:]], axis=0), along_z)
    far_d = move(near_a_d, along_x)

    proj = jnp.concatenate([out_proj, proj_sib], axis=0)
    first_row = lax.axis_index(ALL) * rows
    sib_row = (lax.axis_index(ALL) + sign) * rows
    places = jnp.arange(4, dtype=jnp.int32)
    kinds = jnp.where(places == (x + 1) % 4, 1 - c, c)
    target_table = by_place(targets)
    local_targets = jnp.where(kinds[:, None] == 0, target_table[0], target_table[1])
    local_targets = local_targets.reshape(4, 8, 32).transpose(1, 0, 2).reshape(1, 1024)
    seq_table = by_place(seq_ids).reshape(2, 4, 8, 32).transpose(2, 0, 1, 3).reshape(8, 256)

    hot = hot_rows(jnp.stack([first_row, sib_row]), local_targets, proj.T)

    results = [
        flash(pieces, out_head, head_sib, proj, in_proj)
        for pieces in (
            [hidden],
            [near_a, near_b, near_a_y, near_b_y, near_a_z, near_b_z, far_k, near_a_d],
            [last_y, last_z, far_d],
        )
    ]
    place = jnp.stack(
        [
            k,
            (x + 2 * c) % 4,
            (x - sign + 2 * c + 4) % 4,
            (x - sign + 2 * (1 - c) + 4) % 4,
            (x + 2 + 2 * c) % 4,
        ]
    ).astype(jnp.int32)
    send, side = pack(place, results, hot)
    side_sib = move(side, to_sibling)
    got = lax.all_to_all(send, ALL, 0, 0, tiled=True)
    out = lax.all_to_all(merge(got), ("y", "z"), 0, 0, tiled=True)
    partial = score(kinds.astype(jnp.int32), out, side, side_sib, seq_table, grad_store)
    return finish(lax.all_to_all(partial, ("x", "c"), 0, 0, tiled=True))


def solution(mesh):
    split = Mesh(mesh.devices.reshape(4, 4, 4, 2), ALL)
    everywhere = P(ALL, None)
    return jax.shard_map(
        on_device,
        mesh=split,
        in_specs=(
            P(("x", "c"), None),
            everywhere,
            everywhere,
            P(),
            P(),
            P(),
            P(("y", "z"), ("x", "c")),
        ),
        out_specs=everywhere,
        check_vma=False,
    )
```

time: 243 us -> 146 us (0.60)
  waiting for transfers between devices: 108 us -> 33.1 us
  blocking collectives: 69 us -> 10.2 us
  Pallas kernels: 0 us -> 52.7 us
  matrix products: 43.1 us -> 0 us
  starting transfers between devices: 5.43 us -> 38.2 us
  between operations: 13.6 us -> 0.18 us
  local copies, waits for them, and re-layouts: 1.69 us -> 9.44 us
    all_gather x1 -> x0, waiting for transfers between devices: 90.4 us -> none  [on_device(): tok_piece = lax.all_gather(hidden, FEAT, axis=0, tiled=True)]
    pallas_call x0 -> x8, Pallas kernels: none -> 52.7 us  [the longest x3 41.8 us: flash(): pl.pallas_call(functools.partial(flash_kernel, sizes, tiles), grid=(tiles...]
    dot_general x5 -> x0, matrix products: 43.1 us -> none  [the longest x1 22.8 us: on_device(): lax.dot_general(tok_piece, out_head, (((1,), (1,)), ((), ())), preferred_...]
    all_gather x4 -> x0, blocking collectives: 38.2 us -> none  [all_in_one(): both, at, found = (lax.all_gather(jnp.concatenate(lines), axis), 0, {})]
    ppermute x0 -> x14, starting transfers between devices: none -> 26.9 us  [move(): return lax.ppermute(value, ALL, pairs)]
    all_to_all x2 -> x1, blocking collectives: 30.8 us -> 10.2 us  [on_device(): return finish(lax.all_to_all(partial, ('x', 'c'), 0, 0, tiled=True))]
    ppermute x0 -> x14, waiting for transfers between devices: none -> 11.4 us  [move(): return lax.ppermute(value, ALL, pairs)]
    all_to_all x1 -> x2, starting transfers between devices: 5.43 us -> 11.2 us  [the longest x1 7.73 us: on_device(): got = lax.all_to_all(send, ALL, 0, 0, tiled=True)]
  transfers between devices with their start and end apart: 2 -> 16, of which waited for: 2 -> 4; matrix products, arithmetic and copies ran while one was open for 4% -> 4% of each run, Pallas kernels for 0% -> 22%
where the time goes in v1:
time: 146 us; the launch traced here: 145 us
  Pallas kernels  52.7 us (36%)
  starting transfers between devices  38.2 us (26%)
  waiting for transfers between devices  33.1 us (23%)
  blocking collectives  10.2 us (7%)
  local copies, waits for them, and re-layouts  9.44 us (6%)
    pallas_call x3, Pallas kernels, flash(): pl.pallas_call(functools.partial(flash_kernel, sizes, tiles), grid=(tiles...  41.8 us
    ppermute x14, starting transfers between devices, move(): return lax.ppermute(value, ALL, pairs)  26.9 us
    all_to_all x1, waiting for transfers between devices, on_device(): got = lax.all_to_all(send, ALL, 0, 0, tiled=True)  15.3 us
    ppermute x14, waiting for transfers between devices, move(): return lax.ppermute(value, ALL, pairs)  11.4 us
    all_to_all x1, blocking collectives, on_device(): return finish(lax.all_to_all(partial, ('x', 'c'), 0, 0, tiled=True))  10.2 us
    all_to_all x1, starting transfers between devices, on_device(): got = lax.all_to_all(send, ALL, 0, 0, tiled=True)  7.73 us
    all_to_all x1, waiting for transfers between devices, on_device(): out = lax.all_to_all(merge(got), ('y', 'z'), 0, 0, tiled=True)  6.43 us
    pallas_call x1, Pallas kernels, score(): pl.pallas_call(score_kernel, grid=(8,), in_specs=[pl.BlockSpec(memory_spa...  4.75 us
  transfers between devices with their start and end apart: 16, of which 4 were waited for; matrix products, arithmetic and copies ran while one was open for 4% of the time, Pallas kernels for 22%

profile of v1, /device:TPU:1, one launch (start us, length us, event | category | flops | bytes accessed | tf_op | source)
XLA Modules:
  0.0 145.0 jit_solution(4523385026253597252)
XLA Ops:
  1.4 2.1 %constant_dynamic-slice_fusion = (bf16[64,4096]{1,0:T(8,128)(2,1)S(1)}, bf16[64,4096]{1,0:T(8,128)(2,1)}) fusion(bf16[256,4096]{1,0:T(8,128)(2,1)} %refs_0_.1, s32[]{:T(128)S(6)} %select_n.55, s32[]{:T(128)S(6)} %select_n.54), kind=kLoop, calls=%fused_computation.14 | loop fusion | bytes 2097160 | tf_op jit(solution)/shard_map/dynamic_slice | solution.py:334
  3.5 2.6 %collective-permute-start.2 = (bf16[64,4096]{1,0:T(8,128)(2,1)S(1)}, bf16[64,4096]{1,0:T(8,128)(2,1)S(1)}, u32[]{:S(2)}, u32[]{:S(2)}) collective-permute-start(bf16[64,4096]{1,0:T(8,128)(2,1)S(1)} %get-tuple-element.37), channel_id=1, source_target_pairs={{0,2},{1,7},{2,4},{3,1},{4,6},{5,3},{6,0},{7,5},{8,10},{9,15},{10,... | collective-permute-start | bytes 1572872 | tf_op jit(solution)/shard_map/ppermute | solution.py:30
  7.6 9.1 %collective-permute-done.2.refs_0_ = bf16[64,4096]{1,0:T(8,128)(2,1)S(1)} collective-permute-done((bf16[64,4096]{1,0:T(8,128)(2,1)S(1)}, bf16[64,4096]{1,0:T(8,128)(2,1)S(1)}, u32[]{:S(2)}, u32[]{:S(2)}) %collective-permute-start.2) | collective-permute-done | bytes 524320 | tf_op jit(solution)/shard_map/ppermute | solution.py:30
  16.7 3.1 %collective-permute-start.8 = (bf16[64,4096]{1,0:T(8,128)(2,1)S(1)}, bf16[64,4096]{1,0:T(8,128)(2,1)S(1)}, u32[]{:S(2)}, u32[]{:S(2)}) collective-permute-start(bf16[64,4096]{1,0:T(8,128)(2,1)S(1)} %collective-permute-done.2.refs_0_), channel_id=1, source_target_pairs={{0,2},{1,7},{2,4},{3,1},{4,6},{5,3},{6,0},{7,5},{8,10},{9,15},{10,... | collective-permute-start | bytes 1572872 | tf_op jit(solution)/shard_map/ppermute | solution.py:30
  19.8 2.7 %collective-permute-start.5 = (bf16[64,4096]{1,0:T(8,128)(2,1)}, bf16[64,4096]{1,0:T(8,128)(2,1)S(1)}, u32[]{:S(2)}, u32[]{:S(2)}) collective-permute-start(bf16[64,4096]{1,0:T(8,128)(2,1)} %collective-permute-done.3.refs_1_), channel_id=1, source_target_pairs={{0,32},{1,97},{2,34},{3,99},{4,36},{5,101},{6,38},{7,103},{8,40},{... | collective-permute-start | bytes 1572872 | tf_op jit(solution)/shard_map/ppermute | solution.py:30
  22.6 3.8 %collective-permute-start.7 = (bf16[64,4096]{1,0:T(8,128)(2,1)}, bf16[64,4096]{1,0:T(8,128)(2,1)S(1)}, u32[]{:S(2)}, u32[]{:S(2)}) collective-permute-start(bf16[64,4096]{1,0:T(8,128)(2,1)} %collective-permute-done.3.refs_1_), channel_id=1, source_target_pairs={{0,8},{1,25},{2,10},{3,27},{4,12},{5,29},{6,14},{7,31},{8,16},{9,1... | collective-permute-start | bytes 1572872 | tf_op jit(solution)/shard_map/ppermute | solution.py:30
  29.4 3.4 %collective-permute-start.6 = (bf16[64,4096]{1,0:T(8,128)(2,1)S(1)}, bf16[64,4096]{1,0:T(8,128)(2,1)S(1)}, u32[]{:S(2)}, u32[]{:S(2)}) collective-permute-start(bf16[64,4096]{1,0:T(8,128)(2,1)S(1)} %collective-permute-done.2.refs_0_), channel_id=1, source_target_pairs={{0,8},{1,25},{2,10},{3,27},{4,12},{5,29},{6,14},{7,31},{8,16},{9,1... | collective-permute-start | bytes 1572872 | tf_op jit(solution)/shard_map/ppermute | solution.py:30
  35.5 3.1 %collective-permute-start.10 = (bf16[96,4096]{1,0:T(8,128)(2,1)S(1)}, bf16[96,4096]{1,0:T(8,128)(2,1)S(1)}, u32[]{:S(2)}, u32[]{:S(2)}) collective-permute-start(bf16[96,4096]{1,0:T(8,128)(2,1)S(1)} %get-tuple-element.42), channel_id=1, source_target_pairs={{0,32},{1,97},{2,34},{3,99},{4,36},{5,101},{6,38},{7,103},{8,40},{... | collective-permute-start | bytes 2359304 | tf_op jit(solution)/shard_map/ppermute | solution.py:30
  39.1 2.2 %collective-permute-done.9.refs_7_ = bf16[64,4096]{1,0:T(8,128)(2,1)S(1)} collective-permute-done((bf16[64,4096]{1,0:T(8,128)(2,1)}, bf16[64,4096]{1,0:T(8,128)(2,1)S(1)}, u32[]{:S(2)}, u32[]{:S(2)}) %collective-permute-start.9) | collective-permute-done | bytes 524320 | tf_op jit(solution)/shard_map/ppermute | solution.py:30
  41.3 2.5 %collective-permute-start.12 = (bf16[64,4096]{1,0:T(8,128)(2,1)S(1)}, bf16[64,4096]{1,0:T(8,128)(2,1)S(1)}, u32[]{:S(2)}, u32[]{:S(2)}) collective-permute-start(bf16[64,4096]{1,0:T(8,128)(2,1)S(1)} %collective-permute-done.9.refs_7_), channel_id=1, source_target_pairs={{0,2},{1,7},{2,4},{3,1},{4,6},{5,3},{6,0},{7,5},{8,10},{9,15},{10,... | collective-permute-start | bytes 1572872 | tf_op jit(solution)/shard_map/ppermute | solution.py:30
  43.8 16.7 %shard_map.74 = (f32[512,128]{1,0:T(8,128)S(1)}, f32[512,128]{1,0:T(8,128)S(1)}, f32[512,128]{1,0:T(8,128)S(1)}) custom-call(bf16[64,4096]{1,0:T(8,128)(2,1)S(1)} %collective-permute-done.2.refs_0_, bf16[64,4096]{1,0:T(8,128)(2,1)} %collective-permute-done.3.refs_1_, bf16[64,4096]{1,0:T(8,128)(2,1)S(1)} %collective-permute-done.4.refs_2_, ...), custom_call_target="tpu_custom_call" | custom-call | flops 8589934592 | bytes 16777216 | tf_op jit(solution)/shard_map/pallas_call | solution.py:106
  60.5 12.5 %shard_map.73 = (f32[256,128]{1,0:T(8,128)S(1)}, f32[256,128]{1,0:T(8,128)S(1)}, f32[256,128]{1,0:T(8,128)S(1)}) custom-call(bf16[256,4096]{1,0:T(8,128)(2,1)S(1)} %copy-done.1, bf16[1024,4096]{1,0:T(8,128)(2,1)} %refs_3_.1, bf16[1024,4096]{1,0:T(8,128)(2,1)} %collective-permute-done.refs_2_.refs_9_.refs_4_, ...), custom_call_target="tpu_custom_call" | custom-call | flops 4294967296 | bytes 16777216 | tf_op jit(solution)/shard_map/pallas_call | solution.py:106
  73.1 12.5 %shard_map.75 = (f32[256,128]{1,0:T(8,128)S(1)}, f32[256,128]{1,0:T(8,128)S(1)}, f32[256,128]{1,0:T(8,128)S(1)}) custom-call(bf16[96,4096]{1,0:T(8,128)(2,1)S(1)} %collective-permute-done.10.refs_0_, bf16[96,4096]{1,0:T(8,128)(2,1)S(1)} %collective-permute-done.11.refs_1_, bf16[64,4096]{1,0:T(8,128)(2,1)S(1)} %collective-permute-done.12.refs_2_, ...), custom_call_target="tpu_custom_call" | custom-call | flops 4294967296 | bytes 16777216 | tf_op jit(solution)/shard_map/pallas_call | solution.py:106
  85.6 1.8 %shard_map.77 = (bf16[128,24,128]{2,1,0:T(8,128)(2,1)}, f32[8,4,32,128]{3,2,1,0:T(8,128)S(1)}) custom-call(s32[5]{0:T(128)S(1)} %stack.38.place, f32[256,128]{1,0:T(8,128)S(1)} %get-tuple-element.18.refs_0_, f32[512,128]{1,0:T(8,128)S(1)} %get-tuple-element.21.refs_1_, f32[256,128]{1,0:T(8,128)S(1)} %get-tuple-element.22.refs_2_, ...), custom_call_target="tpu_custom_call" | custom-call | tf_op jit(solution)/shard_map/pallas_call | solution.py:204
  87.4 7.7 %all-to-all-start = ((bf16[128,24,128]{2,1,0:T(8,128)(2,1)}), bf16[128,24,128]{2,1,0:T(8,128)(2,1)S(1)}, u32[]{:S(2)}, u32[]{:S(2)}) async-start(bf16[128,24,128]{2,1,0:T(8,128)(2,1)} %get-tuple-element.29), calls=%async_computation | async-start | bytes 1572864 | tf_op jit(solution)/shard_map/all_to_all | solution.py:383
  96.4 15.3 %all-to-all-done.got_ref = bf16[128,24,128]{2,1,0:T(8,128)(2,1)S(1)} async-done(((bf16[128,24,128]{2,1,0:T(8,128)(2,1)}), bf16[128,24,128]{2,1,0:T(8,128)(2,1)S(1)}, u32[]{:S(2)}, u32[]{:S(2)}) %all-to-all-start) | async-done | bytes 786464 | tf_op jit(solution)/shard_map/all_to_all | solution.py:383
  111.7 1.5 %shard_map.78 = f32[16,8,256]{2,1,0:T(8,128)} custom-call(bf16[128,24,128]{2,1,0:T(8,128)(2,1)S(1)} %all-to-all-done.got_ref), custom_call_target="tpu_custom_call" | custom-call | tf_op jit(solution)/shard_map/pallas_call | solution.py:244
  113.2 3.5 %all-to-all-start.1 = ((f32[16,8,256]{2,1,0:T(8,128)}), f32[16,8,256]{2,1,0:T(8,128)S(1)}, u32[]{:S(2)}, u32[]{:S(2)}) async-start(f32[16,8,256]{2,1,0:T(8,128)} %shard_map.78), calls=%async_computation.1 | async-start | bytes 262144 | tf_op jit(solution)/shard_map/all_to_all | solution.py:384
  117.1 6.4 %all-to-all-done.1.out_ref = f32[16,8,256]{2,1,0:T(8,128)S(1)} async-done(((f32[16,8,256]{2,1,0:T(8,128)}), f32[16,8,256]{2,1,0:T(8,128)S(1)}, u32[]{:S(2)}, u32[]{:S(2)}) %all-to-all-start.1) | async-done | bytes 131104 | tf_op jit(solution)/shard_map/all_to_all | solution.py:384
  123.5 3.4 %copy-done = bf16[2048,2048]{1,0:T(8,128)(2,1)S(1)} copy-done((bf16[2048,2048]{1,0:T(8,128)(2,1)S(1)}, bf16[2048,2048]{1,0:T(8,128)(2,1)}, u32[]{:S(2)}) %copy-start) | copy-done | bytes 8388632
  126.9 4.8 %shard_map.79 = f32[8,16,256]{2,1,0:T(8,128)S(1)} custom-call(s32[4]{0:T(128)S(1)} %get-tuple-element.36.flags, f32[16,8,256]{2,1,0:T(8,128)S(1)} %all-to-all-done.1.out_ref, f32[8,4,32,128]{3,2,1,0:T(8,128)S(1)} %get-tuple-element.30.own_ref, f32[8,4,32,128]{3,2,1,0:T(8,128)S(1)} %collective-permute-done.13.sib_ref, s32[8,256]{1,0:T(8,128)S(1)} %reshape.46.seq_ref, ...), custom_call_target="tpu_custom_call" | custom-call | tf_op jit(solution)/shard_map/pallas_call | solution.py:289
  131.6 10.2 %all_to_all.15.got_ref = f32[8,16,256]{2,1,0:T(8,128)} all-to-all(f32[8,16,256]{2,1,0:T(8,128)S(1)} %shard_map.79), channel_id=1, replica_groups=mesh['y'=4,'z'=4,'x'=4,'c'=2] {'x','c'}, dimensions={0} | all-to-all | bytes 262144 | tf_op jit(solution)/shard_map/all_to_all | solution.py:386
  141.8 1.7 %shard_map.80 = f32[256,16]{1,0:T(8,128)} custom-call(f32[8,16,256]{2,1,0:T(8,128)} %all_to_all.15.got_ref), custom_call_target="tpu_custom_call" | custom-call | tf_op jit(solution)/shard_map/pallas_call | solution.py:315
  143.5 1.6 %copy.29 = f32[256,16]{0,1:T(8,128)} copy(f32[256,16]{1,0:T(8,128)} %shard_map.80) | data formatting | bytes 32768 | tf_op jit(solution)/shard_map/pallas_call | solution.py:315
  (58 shorter events, 10.7 us)
Async XLA Ops:
  0.0 6.3 %copy-start.3 = (bf16[1024,128]{1,0:T(8,128)(2,1)S(1)}, bf16[1024,128]{1,0:T(8,128)(2,1)}, u32[]{:S(2)}) copy-start(bf16[1024,128]{1,0:T(8,128)(2,1)} %param.9) | copy-start | bytes 786436
  0.0 7.3 %copy-start.4 = (s32[2048]{0:T(1024)S(1)}, s32[2048]{0:T(1024)}, u32[]{:S(2)}) copy-start(s32[2048]{0:T(1024)} %param.11) | copy-start | bytes 24580
  0.0 43.8 %collective-permute-start = (bf16[1024,4096]{1,0:T(8,128)(2,1)}, bf16[1024,4096]{1,0:T(8,128)(2,1)}, u32[]{:S(2)}, u32[]{:S(2)}) collective-permute-start(bf16[1024,4096]{1,0:T(8,128)(2,1)} %refs_3_.1), channel_id=1, source_target_pairs={{0,1},{1,0},{2,3},{3,2},{4,5},{5,4},{6,7},{7,6},{8,9},{9,8},{10,11... | collective-permute-start | bytes 25165832 | tf_op jit(solution)/shard_map/ppermute | solution.py:30
  3.5 13.2 %collective-permute-start.2 = (bf16[64,4096]{1,0:T(8,128)(2,1)S(1)}, bf16[64,4096]{1,0:T(8,128)(2,1)S(1)}, u32[]{:S(2)}, u32[]{:S(2)}) collective-permute-start(bf16[64,4096]{1,0:T(8,128)(2,1)S(1)} %get-tuple-element.37), channel_id=1, source_target_pairs={{0,2},{1,7},{2,4},{3,1},{4,6},{5,3},{6,0},{7,5},{8,10},{9,15},{10,... | collective-permute-start | bytes 1572872 | tf_op jit(solution)/shard_map/ppermute | solution.py:30
  6.1 13.7 %collective-permute-start.3 = (bf16[64,4096]{1,0:T(8,128)(2,1)S(1)}, bf16[64,4096]{1,0:T(8,128)(2,1)}, u32[]{:S(2)}, u32[]{:S(2)}) collective-permute-start(bf16[64,4096]{1,0:T(8,128)(2,1)S(1)} %get-tuple-element.37), channel_id=1, source_target_pairs={{0,7},{1,2},{2,1},{3,4},{4,3},{5,6},{6,5},{7,0},{8,15},{9,10},{10,... | collective-permute-start | bytes 1572872 | tf_op jit(solution)/shard_map/ppermute | solution.py:30
  6.5 20.2 %collective-permute-start.1 = (bf16[1024,128]{0,1:T(8,128)(2,1)S(1)}, bf16[1024,128]{0,1:T(8,128)(2,1)S(1)}, u32[]{:S(2)}, u32[]{:S(2)}) collective-permute-start(bf16[1024,128]{0,1:T(8,128)(2,1)S(1)} %copy.23), channel_id=1, source_target_pairs={{0,1},{1,0},{2,3},{3,2},{4,5},{5,4},{6,7},{7,6},{8,9},{9,8},{10,11... | collective-permute-start | bytes 786440 | tf_op jit(solution)/shard_map/ppermute | solution.py:30
  16.7 18.6 %collective-permute-start.8 = (bf16[64,4096]{1,0:T(8,128)(2,1)S(1)}, bf16[64,4096]{1,0:T(8,128)(2,1)S(1)}, u32[]{:S(2)}, u32[]{:S(2)}) collective-permute-start(bf16[64,4096]{1,0:T(8,128)(2,1)S(1)} %collective-permute-done.2.refs_0_), channel_id=1, source_target_pairs={{0,2},{1,7},{2,4},{3,1},{4,6},{5,3},{6,0},{7,5},{8,10},{9,15},{10,... | collective-permute-start | bytes 1572872 | tf_op jit(solution)/shard_map/ppermute | solution.py:30
  19.8 9.6 %collective-permute-start.5 = (bf16[64,4096]{1,0:T(8,128)(2,1)}, bf16[64,4096]{1,0:T(8,128)(2,1)S(1)}, u32[]{:S(2)}, u32[]{:S(2)}) collective-permute-start(bf16[64,4096]{1,0:T(8,128)(2,1)} %collective-permute-done.3.refs_1_), channel_id=1, source_target_pairs={{0,32},{1,97},{2,34},{3,99},{4,36},{5,101},{6,38},{7,103},{8,40},{... | collective-permute-start | bytes 1572872 | tf_op jit(solution)/shard_map/ppermute | solution.py:30
  22.6 10.2 %collective-permute-start.7 = (bf16[64,4096]{1,0:T(8,128)(2,1)}, bf16[64,4096]{1,0:T(8,128)(2,1)S(1)}, u32[]{:S(2)}, u32[]{:S(2)}) collective-permute-start(bf16[64,4096]{1,0:T(8,128)(2,1)} %collective-permute-done.3.refs_1_), channel_id=1, source_target_pairs={{0,8},{1,25},{2,10},{3,27},{4,12},{5,29},{6,14},{7,31},{8,16},{9,1... | collective-permute-start | bytes 1572872 | tf_op jit(solution)/shard_map/ppermute | solution.py:30
  28.8 9.8 %collective-permute-start.4 = (bf16[64,4096]{1,0:T(8,128)(2,1)S(1)}, bf16[64,4096]{1,0:T(8,128)(2,1)S(1)}, u32[]{:S(2)}, u32[]{:S(2)}) collective-permute-start(bf16[64,4096]{1,0:T(8,128)(2,1)S(1)} %collective-permute-done.2.refs_0_), channel_id=1, source_target_pairs={{0,32},{1,97},{2,34},{3,99},{4,36},{5,101},{6,38},{7,103},{8,40},{... | collective-permute-start | bytes 1572872 | tf_op jit(solution)/shard_map/ppermute | solution.py:30
  29.4 14.4 %collective-permute-start.6 = (bf16[64,4096]{1,0:T(8,128)(2,1)S(1)}, bf16[64,4096]{1,0:T(8,128)(2,1)S(1)}, u32[]{:S(2)}, u32[]{:S(2)}) collective-permute-start(bf16[64,4096]{1,0:T(8,128)(2,1)S(1)} %collective-permute-done.2.refs_0_), channel_id=1, source_target_pairs={{0,8},{1,25},{2,10},{3,27},{4,12},{5,29},{6,14},{7,31},{8,16},{9,1... | collective-permute-start | bytes 1572872 | tf_op jit(solution)/shard_map/ppermute | solution.py:30
  32.8 8.5 %collective-permute-start.9 = (bf16[64,4096]{1,0:T(8,128)(2,1)}, bf16[64,4096]{1,0:T(8,128)(2,1)S(1)}, u32[]{:S(2)}, u32[]{:S(2)}) collective-permute-start(bf16[64,4096]{1,0:T(8,128)(2,1)} %get-tuple-element.20), channel_id=1, source_target_pairs={{0,2},{1,7},{2,4},{3,1},{4,6},{5,3},{6,0},{7,5},{8,10},{9,15},{10,... | collective-permute-start | bytes 1572872 | tf_op jit(solution)/shard_map/ppermute | solution.py:30
  35.5 37.5 %collective-permute-start.10 = (bf16[96,4096]{1,0:T(8,128)(2,1)S(1)}, bf16[96,4096]{1,0:T(8,128)(2,1)S(1)}, u32[]{:S(2)}, u32[]{:S(2)}) collective-permute-start(bf16[96,4096]{1,0:T(8,128)(2,1)S(1)} %get-tuple-element.42), channel_id=1, source_target_pairs={{0,32},{1,97},{2,34},{3,99},{4,36},{5,101},{6,38},{7,103},{8,40},{... | collective-permute-start | bytes 2359304 | tf_op jit(solution)/shard_map/ppermute | solution.py:30
  38.6 21.9 %copy-start.1 = (bf16[256,4096]{1,0:T(8,128)(2,1)S(1)}, bf16[256,4096]{1,0:T(8,128)(2,1)}, u32[]{:S(2)}) copy-start(bf16[256,4096]{1,0:T(8,128)(2,1)} %refs_0_.1) | copy-start | bytes 6291460
  38.6 21.9 %copy-start.2 = (bf16[4096,128]{1,0:T(8,128)(2,1)S(1)}, bf16[4096,128]{1,0:T(8,128)(2,1)}, u32[]{:S(2)}) copy-start(bf16[4096,128]{1,0:T(8,128)(2,1)} %refs_6_.1) | copy-start | bytes 3145732
  38.6 34.5 %collective-permute-start.11 = (bf16[96,4096]{1,0:T(8,128)(2,1)S(1)}, bf16[96,4096]{1,0:T(8,128)(2,1)S(1)}, u32[]{:S(2)}, u32[]{:S(2)}) collective-permute-start(bf16[96,4096]{1,0:T(8,128)(2,1)S(1)} %get-tuple-element.41), channel_id=1, source_target_pairs={{0,8},{1,25},{2,10},{3,27},{4,12},{5,29},{6,14},{7,31},{8,16},{9,1... | collective-permute-start | bytes 2359304 | tf_op jit(solution)/shard_map/ppermute | solution.py:30
  41.3 31.8 %collective-permute-start.12 = (bf16[64,4096]{1,0:T(8,128)(2,1)S(1)}, bf16[64,4096]{1,0:T(8,128)(2,1)S(1)}, u32[]{:S(2)}, u32[]{:S(2)}) collective-permute-start(bf16[64,4096]{1,0:T(8,128)(2,1)S(1)} %collective-permute-done.9.refs_7_), channel_id=1, source_target_pairs={{0,2},{1,7},{2,4},{3,1},{4,6},{5,3},{6,0},{7,5},{8,10},{9,15},{10,... | collective-permute-start | bytes 1572872 | tf_op jit(solution)/shard_map/ppermute | solution.py:30
  85.6 10.7 %copy-start.5 = (s32[2048]{0:T(1024)S(1)}, s32[2048]{0:T(1024)}, u32[]{:S(2)}) copy-start(s32[2048]{0:T(1024)} %param.12) | copy-start | bytes 24580
  87.4 24.3 %all-to-all-start = ((bf16[128,24,128]{2,1,0:T(8,128)(2,1)}), bf16[128,24,128]{2,1,0:T(8,128)(2,1)S(1)}, u32[]{:S(2)}, u32[]{:S(2)}) async-start(bf16[128,24,128]{2,1,0:T(8,128)(2,1)} %get-tuple-element.29), calls=%async_computation | async-start | bytes 1572864 | tf_op jit(solution)/shard_map/all_to_all | solution.py:383
  95.2 21.9 %collective-permute-start.13 = (f32[8,4,32,128]{3,2,1,0:T(8,128)S(1)}, f32[8,4,32,128]{3,2,1,0:T(8,128)S(1)}, u32[]{:S(2)}, u32[]{:S(2)}) collective-permute-start(f32[8,4,32,128]{3,2,1,0:T(8,128)S(1)} %get-tuple-element.30.own_ref), channel_id=1, source_target_pairs={{0,1},{1,0},{2,3},{3,2},{4,5},{5,4},{6,7},{7,6},{8,9},{9,8},{10,11... | collective-permute-start | bytes 1572872 | tf_op jit(solution)/shard_map/ppermute | solution.py:30
  113.2 10.3 %all-to-all-start.1 = ((f32[16,8,256]{2,1,0:T(8,128)}), f32[16,8,256]{2,1,0:T(8,128)S(1)}, u32[]{:S(2)}, u32[]{:S(2)}) async-start(f32[16,8,256]{2,1,0:T(8,128)} %shard_map.78), calls=%async_computation.1 | async-start | bytes 262144 | tf_op jit(solution)/shard_map/all_to_all | solution.py:384
  123.5 3.4 %copy-start = (bf16[2048,2048]{1,0:T(8,128)(2,1)S(1)}, bf16[2048,2048]{1,0:T(8,128)(2,1)}, u32[]{:S(2)}) copy-start(bf16[2048,2048]{1,0:T(8,128)(2,1)} %store_ref.1) | copy-start | bytes 25165828

commit v2 on v1

v2 whole, which is shorter than its diff:
```python
import functools

import jax
import jax.numpy as jnp
from jax import lax
from jax.experimental import pallas as pl
from jax.experimental.pallas import tpu as pltpu
from jax.sharding import Mesh
from jax.sharding import PartitionSpec as P

SEQS = 16
ALL = ("y", "z", "x", "c")
TILE = 256
LIMIT = 44 * 1024 * 1024
BF = jnp.bfloat16
F32 = jnp.float32


def index(y, z, x, c):
    return (((y % 4) * 4 + z % 4) * 4 + x % 4) * 2 + c


def move(value, target):
    pairs = [
        (index(y, z, x, c), index(*target(y, z, x, c)))
        for y in range(4)
        for z in range(4)
        for x in range(4)
        for c in range(2)
    ]
    return lax.ppermute(value, ALL, pairs)


def along_x(y, z, x, c):
    return (y, z, x + 1 - 2 * c, c)


def along_x_crossed(y, z, x, c):
    return (y, z, x - 1 + 2 * c, 1 - c)


def along_y(y, z, x, c):
    return (y + 1 - 2 * c, z, x, c)


def along_z(y, z, x, c):
    return (y, z + 1 - 2 * c, x, c)


def to_sibling(y, z, x, c):
    return (y, z, x, 1 - c)


def flash_kernel(sizes, bounds, *refs):
    count = len(sizes)
    pieces, heads = refs[:count], refs[count : count + 2]
    proj_refs, in_ref = refs[count + 2 : count + 4], refs[count + 4]
    out_ref, lse_ref, side_ref = refs[count + 5 : count + 8]
    tok, held, proj, in_proj, scores, piece_sem, head_sem, proj_sem = refs[count + 8 :]
    rows = heads[0].shape[0]

    arrivals = []
    at = 0
    for number, (size, piece) in enumerate(zip(sizes, pieces)):
        arrivals.append(
            pltpu.make_async_copy(piece, tok.at[at : at + size, :], piece_sem.at[number])
        )
        at += size
    blocks = []
    for number, (low, high) in enumerate(zip(bounds, bounds[1:])):
        head, shift = (heads[0], 0) if low < rows else (heads[1], rows)
        blocks.append(
            pltpu.make_async_copy(
                head.at[low - shift : high - shift, :], held.at[low:high, :], head_sem.at[number]
            )
        )
    others = [
        pltpu.make_async_copy(proj_refs[0], proj.at[0:rows, :], proj_sem.at[0]),
        pltpu.make_async_copy(proj_refs[1], proj.at[rows : 2 * rows, :], proj_sem.at[1]),
        pltpu.make_async_copy(in_ref, in_proj, proj_sem.at[2]),
    ]
    for copy in arrivals + blocks + others:
        copy.start()
    for copy in arrivals:
        copy.wait()

    dims = (((1,), (1,)), ((), ()))
    for block, low, high in zip(blocks, bounds, bounds[1:]):
        block.wait()
        scores[:, low:high] = lax.dot_general(
            tok[...], held[low:high, :], dims, preferred_element_type=F32
        )
    for copy in others:
        copy.wait()
    side_ref[...] = jnp.dot(tok[...], in_proj[...], preferred_element_type=F32)

    step = 512
    best = scores[:, 0:step]
    for low in range(step, 2 * rows, step):
        best = jnp.maximum(best, scores[:, low : low + step])
    best = jnp.max(best, axis=1, keepdims=True)
    total = None
    mixed = None
    for low in range(0, 2 * rows, step):
        power = jnp.exp(scores[:, low : low + step] - best)
        total = power if low == 0 else total + power
        part = jnp.dot(
            power.astype(BF), proj[low : low + step, :], preferred_element_type=F32
        )
        mixed = part if low == 0 else mixed + part
    total = jnp.sum(total, axis=1, keepdims=True)
    out_ref[...] = mixed / total
    lse_ref[...] = jnp.broadcast_to(best + jnp.log(total), lse_ref.shape)


def flash(pieces, own, sib, proj_own, proj_sib, in_proj):
    sizes = tuple(p.shape[0] for p in pieces)
    n = sum(sizes)
    rows, depth = own.shape
    rank = proj_own.shape[1]
    bounds = (0, 256, 512, 1024, 1536, 2048)
    here = pl.BlockSpec(memory_space=pltpu.VMEM)
    away = pl.BlockSpec(memory_space=pl.ANY)
    return pl.pallas_call(
        functools.partial(flash_kernel, sizes, bounds),
        in_specs=[away] * (len(pieces) + 5),
        out_specs=[here] * 3,
        out_shape=[jax.ShapeDtypeStruct((n, rank), F32)] * 3,
        scratch_shapes=[
            pltpu.VMEM((n, depth), BF),
            pltpu.VMEM((2 * rows, depth), BF),
            pltpu.VMEM((2 * rows, rank), BF),
            pltpu.VMEM(in_proj.shape, BF),
            pltpu.VMEM((n, 2 * rows), F32),
            pltpu.SemaphoreType.DMA((len(pieces),)),
            pltpu.SemaphoreType.DMA((len(bounds) - 1,)),
            pltpu.SemaphoreType.DMA((3,)),
        ],
        compiler_params=pltpu.CompilerParams(vmem_limit_bytes=LIMIT),
        cost_estimate=pl.CostEstimate(
            flops=2 * n * 2 * rows * depth, bytes_accessed=2 * rows * depth * 2, transcendentals=0
        ),
    )(*pieces, own, sib, proj_own, proj_sib, in_proj)


def hot_kernel(where, targets_ref, own_ref, sib_ref, out_ref):
    local = out_ref.shape[1]
    total = jnp.zeros(out_ref.shape, F32)
    for which, proj_ref in enumerate((own_ref, sib_ref)):
        for first in range(0, proj_ref.shape[0], TILE):
            ids = where[which] + first + lax.broadcasted_iota(jnp.int32, (TILE, local), 0)
            hot = jnp.where(ids == targets_ref[...], 1.0, 0.0).astype(BF)
            total += lax.dot_general(
                proj_ref[first : first + TILE, :],
                hot,
                (((0,), (0,)), ((), ())),
                preferred_element_type=F32,
            )
    out_ref[...] = total


def hot_rows(where, targets, proj_own, proj_sib):
    here = pl.BlockSpec(memory_space=pltpu.VMEM)
    return pl.pallas_call(
        hot_kernel,
        in_specs=[pl.BlockSpec(memory_space=pltpu.SMEM), here, here, here],
        out_specs=here,
        out_shape=jax.ShapeDtypeStruct((proj_own.shape[1], targets.shape[1]), F32),
        compiler_params=pltpu.CompilerParams(vmem_limit_bytes=16 * 1024 * 1024),
        cost_estimate=pl.CostEstimate(
            flops=2 * 128 * 2048 * 1024, bytes_accessed=1 << 20, transcendentals=0
        ),
    )(where, targets, proj_own, proj_sib)


def pack_kernel(place, *refs):
    outs, lses, sides = refs[0:3], refs[3:6], refs[6:9]
    hot_ref, send_ref, side_ref, out_nat, lse_nat = refs[9:]
    k = place[0]
    spot = [place[1], place[2], place[3], place[4]]

    def put(slot, quarter, source, start, rows, into=0):
        for h in range(rows // 32):
            group = quarter * 2 + into + h
            at = slice(start + 32 * h, start + 32 * h + 32)
            out_nat[group, spot[slot]] = outs[source][at, :]
            lse_nat[group, spot[slot]] = lses[source][at, :]
            side_ref[group, spot[slot]] = sides[source][at, :]

    ky, kz, kd = k ^ 2, k ^ 1, k ^ 3
    for q in range(4):
        put(0, q, 0, 64 * q, 64)
    for n, (slot, quarter) in enumerate(
        [(1, k), (2, k), (1, ky), (2, ky), (1, kz), (2, kz), (3, k), (1, kd)]
    ):
        put(slot, quarter, 1, 64 * n, 64)
    put(3, ky, 2, 0, 64)
    put(2, kd, 2, 64, 32)
    put(3, kz, 2, 96, 64)
    put(2, kd, 2, 160, 32, into=1)
    put(3, kd, 2, 192, 64)

    for group in range(8):
        mixed = jnp.transpose(out_nat[group].reshape(128, 128)).reshape(16, 8, 128)
        lse = jnp.transpose(lse_nat[group].reshape(128, 128))[0:8, :]
        high = lse.astype(BF).astype(F32)
        rest = lse - high
        middle = rest.astype(BF).astype(F32)
        low = rest - middle
        line = lax.broadcasted_iota(jnp.int32, (8, 128), 0)
        stats = jnp.where(
            line == 0, high, jnp.where(line == 1, middle, jnp.where(line == 2, low, 0.0))
        )
        hot = hot_ref[:, group * 128 : group * 128 + 128].reshape(16, 8, 128)
        for part in range(16):
            to = (2 * group + part % 2) * 8 + part // 2
            send_ref[to] = jnp.concatenate([mixed[part], hot[part], stats], axis=0).astype(BF)


def pack(place, results, hot):
    outs, lses, sides = zip(*results)
    return pl.pallas_call(
        pack_kernel,
        in_specs=[pl.BlockSpec(memory_space=pltpu.SMEM)]
        + [pl.BlockSpec(memory_space=pltpu.VMEM)] * 10,
        out_specs=[pl.BlockSpec(memory_space=pltpu.VMEM)] * 2,
        out_shape=[
            jax.ShapeDtypeStruct((128, 24, 128), BF),
            jax.ShapeDtypeStruct((8, 4, 32, 128), F32),
        ],
        scratch_shapes=[pltpu.VMEM((8, 4, 32, 128), F32)] * 2,
        compiler_params=pltpu.CompilerParams(vmem_limit_bytes=16 * 1024 * 1024),
    )(place, *outs, *lses, *sides, hot)


def merge_kernel(got_ref, out_ref):
    lse = (
        got_ref[:, 16:24, :].astype(F32)
    )
    lse = lse[:, 0:1, :] + lse[:, 1:2, :] + lse[:, 2:3, :]
    source = lax.broadcasted_iota(jnp.int32, (128, 1, 128), 0)
    lane = lax.broadcasted_iota(jnp.int32, (128, 1, 128), 2)
    x = lax.div(lax.rem(source, 8), 2)
    c = lax.rem(source, 2)
    other = lax.div(lane, 32) == lax.rem(x + 1, 4)
    kind = jnp.where(other, 1 - c, c)
    halves = []
    for which in range(2):
        mine = kind == which
        best = jnp.max(jnp.where(mine, lse, -3.0e38), axis=0, keepdims=True)
        weight = jnp.where(mine, jnp.exp(jnp.minimum(lse - best, 0.0)), 0.0)
        total = jnp.sum(weight, axis=0)
        mixed = jnp.sum(weight * got_ref[:, 0:8, :].astype(F32), axis=0)
        hot = jnp.sum(jnp.where(mine, got_ref[:, 8:16, :].astype(F32), 0.0), axis=0)
        halves.append(mixed / total - hot)
    both = jnp.concatenate(halves, axis=1)
    for copy in range(16):
        out_ref[copy] = both


def merge(got):
    return pl.pallas_call(
        merge_kernel,
        in_specs=[pl.BlockSpec(memory_space=pltpu.VMEM)],
        out_specs=pl.BlockSpec(memory_space=pltpu.VMEM),
        out_shape=jax.ShapeDtypeStruct((16, 8, 256), F32),
        compiler_params=pltpu.CompilerParams(vmem_limit_bytes=16 * 1024 * 1024),
    )(got)


def score_kernel(flags, out_ref, own_ref, sib_ref, seq_ref, store_ref, result_ref, store, sems):
    rows = store.shape[0] // 8
    copies = [
        pltpu.make_async_copy(
            store_ref.at[n * rows : (n + 1) * rows, :],
            store.at[n * rows : (n + 1) * rows, :],
            sems.at[n],
        )
        for n in range(8)
    ]
    for copy in copies:
        copy.start()
    total = jnp.zeros((256, 128), F32)
    for group in range(8):
        out = jnp.concatenate([out_ref[2 * group], out_ref[2 * group + 1]], axis=0)
        ids = seq_ref[group : group + 1, :]
        member = lax.broadcasted_iota(jnp.int32, (16, 256), 0) == ids
        spread = jnp.where(member[None, :, :], out[:, None, :], 0.0).reshape(256, 256)
        first, second = [], []
        for spot in range(4):
            own, sib = own_ref[group, spot], sib_ref[group, spot]
            keep = flags[spot] == 0
            first.append(jnp.where(keep, own, sib))
            second.append(jnp.where(keep, sib, own))
        side = jnp.concatenate(first + second, axis=0)
        spread_high = spread.astype(BF)
        spread_low = (spread - spread_high.astype(F32)).astype(BF)
        side_high = side.astype(BF)
        side_low = (side - side_high.astype(F32)).astype(BF)
        for a, b in (
            (spread_high, side_high),
            (spread_high, side_low),
            (spread_low, side_high),
        ):
            total += jnp.dot(a, b, preferred_element_type=F32)
    grads = jnp.concatenate(
        [total[i * 16 : (i + 1) * 16, :].astype(BF) for i in range(16)], axis=1
    )
    for n, copy in enumerate(copies):
        copy.wait()
        result_ref[n] = lax.dot_general(
            grads,
            store[n * rows : (n + 1) * rows, :],
            (((1,), (1,)), ((), ())),
            preferred_element_type=F32,
        )


def score(flags, out, own, sib, seq, store):
    here = pl.BlockSpec(memory_space=pltpu.VMEM)
    return pl.pallas_call(
        score_kernel,
        in_specs=[
            pl.BlockSpec(memory_space=pltpu.SMEM),
            here,
            here,
            here,
            here,
            pl.BlockSpec(memory_space=pl.ANY),
        ],
        out_specs=here,
        out_shape=jax.ShapeDtypeStruct((8, SEQS, store.shape[0] // 8), F32),
        scratch_shapes=[pltpu.VMEM(store.shape, BF), pltpu.SemaphoreType.DMA((8,))],
        compiler_params=pltpu.CompilerParams(vmem_limit_bytes=50 * 1024 * 1024),
    )(flags, out, own, sib, seq, store)


def finish_kernel(got_ref, out_ref):
    total = got_ref[0]
    for source in range(1, 8):
        total = total + got_ref[source]
    out_ref[...] = total


def finish(got):
    return pl.pallas_call(
        finish_kernel,
        in_specs=[pl.BlockSpec(memory_space=pltpu.VMEM)],
        out_specs=pl.BlockSpec(memory_space=pltpu.VMEM),
        out_shape=jax.ShapeDtypeStruct((SEQS, 256), F32),
    )(got)


def by_place(per_token):
    table = per_token.reshape(4, 2, 256)
    return jnp.stack([table[:, 0], jnp.roll(table[:, 1], 2, axis=0)])


def on_device(hidden, out_head, out_proj, in_proj, targets, seq_ids, grad_store):
    y, z, x, c = (lax.axis_index(name) for name in ALL)
    k = 2 * (y % 2) + z % 2
    sign = 1 - 2 * c
    rows = out_head.shape[0]

    mine = lax.dynamic_slice_in_dim(hidden, k * 64, 64, 0)

    near_a = move(mine, along_x)
    near_b = move(mine, along_x_crossed)
    head_sib = move(out_head, to_sibling)
    proj_sib = move(out_proj, to_sibling)
    again, proj_sib = lax.optimization_barrier((hidden, proj_sib))
    mine_d = lax.dynamic_slice_in_dim(again, (3 - k) * 64, 64, 0)
    mine_d, near_a, head_sib = lax.optimization_barrier((mine_d, near_a, head_sib))
    far_k = move(near_a, along_x)
    near_a_d = move(mine_d, along_x)
    near = jnp.concatenate([near_a, near_b], axis=0)
    near_y = move(near, along_y)
    near_z = move(near, along_z)
    rest = (out_head, head_sib, out_proj, proj_sib, in_proj)
    first = flash([hidden], *rest)
    first, far_k, near_y, near_z = lax.optimization_barrier((first, far_k, near_y, near_z))
    last_y = move(jnp.concatenate([far_k, near_z[64:96]], axis=0), along_y)
    last_z = move(jnp.concatenate([far_k, near_y[96:128]], axis=0), along_z)
    far_d = move(near_a_d, along_x)

    first_row = lax.axis_index(ALL) * rows
    sib_row = (lax.axis_index(ALL) + sign) * rows
    places = jnp.arange(4, dtype=jnp.int32)
    kinds = jnp.where(places == (x + 1) % 4, 1 - c, c)
    target_table = by_place(targets)
    local_targets = jnp.where(kinds[:, None] == 0, target_table[0], target_table[1])
    local_targets = local_targets.reshape(4, 8, 32).transpose(1, 0, 2).reshape(1, 1024)
    seq_table = by_place(seq_ids).reshape(2, 4, 8, 32).transpose(2, 0, 1, 3).reshape(8, 256)

    hot = hot_rows(jnp.stack([first_row, sib_row]), local_targets, out_proj, proj_sib)

    second = flash([near, near_y, near_z, far_k, near_a_d], *rest)
    third = flash([last_y, last_z, far_d], *rest)
    place = jnp.stack(
        [
            k,
            (x + 2 * c) % 4,
            (x - sign + 2 * c + 4) % 4,
            (x - sign + 2 * (1 - c) + 4) % 4,
            (x + 2 + 2 * c) % 4,
        ]
    ).astype(jnp.int32)
    send, side = pack(place, (first, second, third), hot)
    side_sib = move(side, to_sibling)
    got = lax.all_to_all(send, ALL, 0, 0, tiled=True)
    out = lax.all_to_all(merge(got), ("y", "z"), 0, 0, tiled=True)
    partial = score(kinds.astype(jnp.int32), out, side, side_sib, seq_table, grad_store)
    return finish(lax.all_to_all(partial, ("x", "c"), 0, 0, tiled=True)).T


def solution(mesh):
    split = Mesh(mesh.devices.reshape(4, 4, 4, 2), ALL)
    everywhere = P(ALL, None)
    return jax.shard_map(
        on_device,
        mesh=split,
        in_specs=(
            P(("x", "c"), None),
            everywhere,
            everywhere,
            P(),
            P(),
            P(),
            P(("y", "z"), ("x", "c")),
        ),
        out_specs=everywhere,
        check_vma=False,
    )
```

time: 146 us -> 132 us (0.904)
  starting transfers between devices: 38.2 us -> 29.4 us
  waiting for transfers between devices: 33.1 us -> 29 us
  Pallas kernels: 52.7 us -> 49.1 us
  local copies, waits for them, and re-layouts: 9.44 us -> 12.7 us
    ppermute x14 -> x12, starting transfers between devices: 26.9 us -> 19.1 us  [move(): return lax.ppermute(value, ALL, pairs)]
    ppermute x14 -> x12, waiting for transfers between devices: 11.4 us -> 7.26 us  [move(): return lax.ppermute(value, ALL, pairs)]
    pallas_call x4, Pallas kernels: 46.5 us -> 43 us  [the longest x3 35.2 us: flash(): pl.pallas_call(functools.partial(flash_kernel, sizes, bounds), in_specs=[...]
    slice x2, local copies, waits for them, and re-layouts: 0.04 us -> 1.94 us  [the longest x1 0.97 us: on_device(): last_z = move(jnp.concatenate([far_k, near_y[96:128]], axis=0), along_z)]
    dynamic_slice x0 -> x1, local copies, waits for them, and re-layouts: none -> 1.87 us  [on_device(): mine_d = lax.dynamic_slice_in_dim(again, (3 - k) * 64, 64, 0)]
    pallas_call x1 -> x0, local copies, waits for them, and re-layouts: 1.58 us -> none  [finish(): pl.pallas_call(finish_kernel, in_specs=[pl.BlockSpec(memory_space=pltpu.V...]
    unnamed x13 -> x15, local copies, waits for them, and re-layouts: 3.55 us -> 3.56 us
  transfers between devices with their start and end apart: 16 -> 14, of which waited for: 4 -> 5; matrix products, arithmetic and copies ran while one was open for 4% -> 7% of each run, Pallas kernels for 22% -> 22%
where the time goes in v2:
time: 132 us; the launch traced here: 131 us
  Pallas kernels  49.1 us (37%)
  starting transfers between devices  29.4 us (22%)
  waiting for transfers between devices  29 us (22%)
  local copies, waits for them, and re-layouts  12.7 us (10%)
  blocking collectives  10.2 us (8%)
    pallas_call x3, Pallas kernels, flash(): pl.pallas_call(functools.partial(flash_kernel, sizes, bounds), in_specs=[...  35.2 us
    ppermute x12, starting transfers between devices, move(): return lax.ppermute(value, ALL, pairs)  19.1 us
    all_to_all x1, waiting for transfers between devices, on_device(): got = lax.all_to_all(send, ALL, 0, 0, tiled=True)  15.3 us
    all_to_all x1, blocking collectives, on_device(): return finish(lax.all_to_all(partial, ('x', 'c'), 0, 0, tiled=True)).T  10.2 us
    pallas_call x1, Pallas kernels, score(): pl.pallas_call(score_kernel, in_specs=[pl.BlockSpec(memory_space=pltpu.SM...  7.87 us
    ppermute x12, waiting for transfers between devices, move(): return lax.ppermute(value, ALL, pairs)  7.26 us
    all_to_all x1, starting transfers between devices, on_device(): got = lax.all_to_all(send, ALL, 0, 0, tiled=True)  6.78 us
    all_to_all x1, waiting for transfers between devices, on_device(): out = lax.all_to_all(merge(got), ('y', 'z'), 0, 0, tiled=True)  6.43 us
  transfers between devices with their start and end apart: 14, of which 5 were waited for; matrix products, arithmetic and copies ran while one was open for 7% of the time, Pallas kernels for 22%

profile of v2, /device:TPU:1, one launch (start us, length us, event | category | flops | bytes accessed | tf_op | source)
XLA Modules:
  0.0 131.0 jit_solution(1718483741459730868)
XLA Ops:
  0.0 1.4 %collective-permute-start.2 = (bf16[1024,4096]{1,0:T(8,128)(2,1)}, bf16[1024,4096]{1,0:T(8,128)(2,1)}, u32[]{:S(2)}, u32[]{:S(2)}) collective-permute-start(bf16[1024,4096]{1,0:T(8,128)(2,1)} %refs_3_.3), channel_id=1, source_target_pairs={{0,1},{1,0},{2,3},{3,2},{4,5},{5,4},{6,7},{7,6},{8,9},{9,8},{10,11... | collective-permute-start | bytes 25165832 | tf_op jit(solution)/shard_map/ppermute | solution.py:31
  1.4 2.0 %constant_dynamic-slice_fusion = bf16[64,4096]{1,0:T(8,128)(2,1)} fusion(bf16[256,4096]{1,0:T(8,128)(2,1)} %refs_0_.1, s32[]{:T(128)S(6)} %select_n.55), kind=kLoop, calls=%fused_computation.15 | loop fusion | bytes 1048580 | tf_op jit(solution)/shard_map/dynamic_slice | solution.py:365
  3.4 2.6 %collective-permute-start.1 = (bf16[64,4096]{1,0:T(8,128)(2,1)}, bf16[64,4096]{1,0:T(8,128)(2,1)}, u32[]{:S(2)}, u32[]{:S(2)}) collective-permute-start(bf16[64,4096]{1,0:T(8,128)(2,1)} %constant_dynamic-slice_fusion), channel_id=1, source_target_pairs={{0,2},{1,7},{2,4},{3,1},{4,6},{5,3},{6,0},{7,5},{8,10},{9,15},{10,... | collective-permute-start | bytes 1572872 | tf_op jit(solution)/shard_map/ppermute | solution.py:31
  8.8 1.9 %constant_dynamic-slice_fusion.1 = bf16[64,4096]{1,0:T(8,128)(2,1)} fusion(bf16[256,4096]{1,0:T(8,128)(2,1)} %refs_0_.1, s32[]{:T(128)S(6)} %select_n.54), kind=kLoop, calls=%fused_computation.16 | loop fusion | bytes 1048580 | tf_op jit(solution)/shard_map/dynamic_slice | solution.py:372
  10.7 6.2 %collective-permute-done.1 = bf16[64,4096]{1,0:T(8,128)(2,1)} collective-permute-done((bf16[64,4096]{1,0:T(8,128)(2,1)}, bf16[64,4096]{1,0:T(8,128)(2,1)}, u32[]{:S(2)}, u32[]{:S(2)}) %collective-permute-start.1) | collective-permute-done | bytes 524320 | tf_op jit(solution)/shard_map/ppermute | solution.py:31
  16.9 1.9 %constant_dynamic-update-slice_fusion.1 = bf16[128,4096]{1,0:T(8,128)(2,1)} fusion(bf16[64,4096]{1,0:T(8,128)(2,1)} %collective-permute-done.1), kind=kLoop, calls=%fused_computation.6 | loop fusion | bytes 1048576
  18.7 1.9 %constant_dynamic-update-slice_fusion.refs_0_ = bf16[128,4096]{1,0:T(8,128)(2,1)} fusion(bf16[128,4096]{1,0:T(8,128)(2,1)} %constant_dynamic-update-slice_fusion.1, bf16[64,4096]{1,0:T(8,128)(2,1)} %collective-permute-done.4), kind=kLoop, calls=%fused_computation.5 | loop fusion | bytes 1048576 | tf_op jit(solution)/shard_map/concatenate | solution.py:376
  20.6 2.7 %collective-permute-start.5 = (bf16[128,4096]{1,0:T(8,128)(2,1)}, bf16[128,4096]{1,0:T(8,128)(2,1)}, u32[]{:S(2)}, u32[]{:S(2)}) collective-permute-start(bf16[128,4096]{1,0:T(8,128)(2,1)} %constant_dynamic-update-slice_fusion.refs_0_), channel_id=1, source_target_pairs={{0,32},{1,97},{2,34},{3,99},{4,36},{5,101},{6,38},{7,103},{8,40},{... | collective-permute-start | bytes 3145736 | tf_op jit(solution)/shard_map/ppermute | solution.py:31
  23.3 3.8 %collective-permute-start.6 = (bf16[128,4096]{1,0:T(8,128)(2,1)}, bf16[128,4096]{1,0:T(8,128)(2,1)}, u32[]{:S(2)}, u32[]{:S(2)}) collective-permute-start(bf16[128,4096]{1,0:T(8,128)(2,1)} %constant_dynamic-update-slice_fusion.refs_0_), channel_id=1, source_target_pairs={{0,8},{1,25},{2,10},{3,27},{4,12},{5,29},{6,14},{7,31},{8,16},{9,1... | collective-permute-start | bytes 3145736 | tf_op jit(solution)/shard_map/ppermute | solution.py:31
  27.7 3.1 %collective-permute-start.3 = (bf16[64,4096]{1,0:T(8,128)(2,1)}, bf16[64,4096]{1,0:T(8,128)(2,1)S(1)}, u32[]{:S(2)}, u32[]{:S(2)}) collective-permute-start(bf16[64,4096]{1,0:T(8,128)(2,1)} %collective-permute-done.1), channel_id=1, source_target_pairs={{0,2},{1,7},{2,4},{3,1},{4,6},{5,3},{6,0},{7,5},{8,10},{9,15},{10,... | collective-permute-start | bytes 1572872 | tf_op jit(solution)/shard_map/ppermute | solution.py:31
  31.9 1.3 shard_map.76.refs_9_
  33.3 9.4 %shard_map.73 = (f32[256,128]{1,0:T(8,128)S(1)}, f32[256,128]{1,0:T(8,128)S(1)}, f32[256,128]{1,0:T(8,128)S(1)}) custom-call(bf16[256,4096]{1,0:T(8,128)(2,1)S(1)} %copy-done, bf16[1024,4096]{1,0:T(8,128)(2,1)} %refs_3_.3, bf16[1024,4096]{1,0:T(8,128)(2,1)} %collective-permute-done.2.refs_2_.refs_6_.refs_4_, bf16[1024,128]{1,0:T(8,128)(2,1)S(1)} %copy-done.2, ...), custom_call_target="tpu_custom_call" | custom-call | flops 4294967296 | bytes 16777216 | tf_op jit(solution)/shard_map/pallas_call | solution.py:124
  42.9 3.0 %collective-permute-start.10 = (bf16[64,4096]{1,0:T(8,128)(2,1)S(1)}, bf16[64,4096]{1,0:T(8,128)(2,1)S(1)}, u32[]{:S(2)}, u32[]{:S(2)}) collective-permute-start(bf16[64,4096]{1,0:T(8,128)(2,1)S(1)} %collective-permute-done.7.refs_4_), channel_id=1, source_target_pairs={{0,2},{1,7},{2,4},{3,1},{4,6},{5,3},{6,0},{7,5},{8,10},{9,15},{10,... | collective-permute-start | bytes 1572872 | tf_op jit(solution)/shard_map/ppermute | solution.py:31
  48.7 16.3 %shard_map.74 = (f32[512,128]{1,0:T(8,128)S(1)}, f32[512,128]{1,0:T(8,128)S(1)}, f32[512,128]{1,0:T(8,128)S(1)}) custom-call(bf16[128,4096]{1,0:T(8,128)(2,1)} %constant_dynamic-update-slice_fusion.refs_0_, bf16[128,4096]{1,0:T(8,128)(2,1)} %collective-permute-done.5.refs_1_, bf16[128,4096]{1,0:T(8,128)(2,1)} %collective-permute-done.6.refs_2_, ...), custom_call_target="tpu_custom_call" | custom-call | flops 8589934592 | bytes 16777216 | tf_op jit(solution)/shard_map/pallas_call | solution.py:124
  65.1 9.4 %shard_map.75 = (f32[256,128]{1,0:T(8,128)S(1)}, f32[256,128]{1,0:T(8,128)S(1)}, f32[256,128]{1,0:T(8,128)S(1)}) custom-call(bf16[96,4096]{1,0:T(8,128)(2,1)S(1)} %collective-permute-done.8.refs_0_, bf16[96,4096]{1,0:T(8,128)(2,1)S(1)} %collective-permute-done.9.refs_1_, bf16[64,4096]{1,0:T(8,128)(2,1)S(1)} %collective-permute-done.10.refs_2_, ...), custom_call_target="tpu_custom_call" | custom-call | flops 4294967296 | bytes 16777216 | tf_op jit(solution)/shard_map/pallas_call | solution.py:124
  74.5 1.8 %shard_map.77 = (bf16[128,24,128]{2,1,0:T(8,128)(2,1)}, f32[8,4,32,128]{3,2,1,0:T(8,128)S(1)}) custom-call(s32[5]{0:T(128)S(1)} %stack.38.place, f32[256,128]{1,0:T(8,128)S(1)} %get-tuple-element.34.refs_0_, f32[512,128]{1,0:T(8,128)S(1)} %get-tuple-element.39.refs_1_, f32[256,128]{1,0:T(8,128)S(1)} %get-tuple-element.40.refs_2_, ...), custom_call_target="tpu_custom_call" | custom-call | tf_op jit(solution)/shard_map/pallas_call | solution.py:222
  76.3 6.8 %all-to-all-start = ((bf16[128,24,128]{2,1,0:T(8,128)(2,1)}), bf16[128,24,128]{2,1,0:T(8,128)(2,1)S(1)}, u32[]{:S(2)}, u32[]{:S(2)}) async-start(bf16[128,24,128]{2,1,0:T(8,128)(2,1)} %get-tuple-element.47), calls=%async_computation | async-start | bytes 1572864 | tf_op jit(solution)/shard_map/all_to_all | solution.py:410
  84.3 15.3 %all-to-all-done.got_ref = bf16[128,24,128]{2,1,0:T(8,128)(2,1)S(1)} async-done(((bf16[128,24,128]{2,1,0:T(8,128)(2,1)}), bf16[128,24,128]{2,1,0:T(8,128)(2,1)S(1)}, u32[]{:S(2)}, u32[]{:S(2)}) %all-to-all-start) | async-done | bytes 786464 | tf_op jit(solution)/shard_map/all_to_all | solution.py:410
  99.6 1.4 %shard_map.78 = f32[16,8,256]{2,1,0:T(8,128)} custom-call(bf16[128,24,128]{2,1,0:T(8,128)(2,1)S(1)} %all-to-all-done.got_ref), custom_call_target="tpu_custom_call" | custom-call | tf_op jit(solution)/shard_map/pallas_call | solution.py:262
  101.1 3.5 %all-to-all-start.1 = ((f32[16,8,256]{2,1,0:T(8,128)}), f32[16,8,256]{2,1,0:T(8,128)S(1)}, u32[]{:S(2)}, u32[]{:S(2)}) async-start(f32[16,8,256]{2,1,0:T(8,128)} %shard_map.78), calls=%async_computation.1 | async-start | bytes 262144 | tf_op jit(solution)/shard_map/all_to_all | solution.py:411
  105.0 6.4 %all-to-all-done.1.out_ref = f32[16,8,256]{2,1,0:T(8,128)S(1)} async-done(((f32[16,8,256]{2,1,0:T(8,128)}), f32[16,8,256]{2,1,0:T(8,128)S(1)}, u32[]{:S(2)}, u32[]{:S(2)}) %all-to-all-start.1) | async-done | bytes 131104 | tf_op jit(solution)/shard_map/all_to_all | solution.py:411
  111.4 7.9 %shard_map.79 = f32[8,16,256]{2,1,0:T(8,128)S(1)} custom-call(s32[4]{0:T(128)S(1)} %get-tuple-element.54.flags, f32[16,8,256]{2,1,0:T(8,128)S(1)} %all-to-all-done.1.out_ref, f32[8,4,32,128]{3,2,1,0:T(8,128)S(1)} %get-tuple-element.48.own_ref, f32[8,4,32,128]{3,2,1,0:T(8,128)S(1)} %collective-permute-done.11.sib_ref, s32[8,256]{1,0:T(8,128)S(1)} %reshape.46.seq_ref, ...), custom_call_target="tpu_custom_call" | custom-call | tf_op jit(solution)/shard_map/pallas_call | solution.py:321
  119.3 10.2 %all_to_all.15.got_ref = f32[8,16,256]{2,1,0:T(8,128)} all-to-all(f32[8,16,256]{2,1,0:T(8,128)S(1)} %shard_map.79), channel_id=1, replica_groups=mesh['y'=4,'z'=4,'x'=4,'c'=2] {'x','c'}, dimensions={0} | all-to-all | bytes 262144 | tf_op jit(solution)/shard_map/all_to_all | solution.py:413
  129.4 1.5 %shard_map.80 = f32[16,256]{1,0:T(8,128)} custom-call(f32[8,16,256]{2,1,0:T(8,128)} %all_to_all.15.got_ref), custom_call_target="tpu_custom_call" | custom-call | tf_op jit(solution)/shard_map/pallas_call | solution.py:346
  (55 shorter events, 9.1 us)
Async XLA Ops:
  0.0 16.9 %collective-permute-start.2 = (bf16[1024,4096]{1,0:T(8,128)(2,1)}, bf16[1024,4096]{1,0:T(8,128)(2,1)}, u32[]{:S(2)}, u32[]{:S(2)}) collective-permute-start(bf16[1024,4096]{1,0:T(8,128)(2,1)} %refs_3_.3), channel_id=1, source_target_pairs={{0,1},{1,0},{2,3},{3,2},{4,5},{5,4},{6,7},{7,6},{8,9},{9,8},{10,11... | collective-permute-start | bytes 25165832 | tf_op jit(solution)/shard_map/ppermute | solution.py:31
  1.4 6.7 %collective-permute-start = (bf16[1024,128]{1,0:T(8,128)(2,1)}, bf16[1024,128]{1,0:T(8,128)(2,1)S(1)}, u32[]{:S(2)}, u32[]{:S(2)}) collective-permute-start(bf16[1024,128]{1,0:T(8,128)(2,1)} %own_ref.1), channel_id=1, source_target_pairs={{0,1},{1,0},{2,3},{3,2},{4,5},{5,4},{6,7},{7,6},{8,9},{9,8},{10,11... | collective-permute-start | bytes 786440 | tf_op jit(solution)/shard_map/ppermute | solution.py:31
  1.4 29.6 %copy-start.2 = (bf16[1024,128]{1,0:T(8,128)(2,1)S(1)}, bf16[1024,128]{1,0:T(8,128)(2,1)}, u32[]{:S(2)}) copy-start(bf16[1024,128]{1,0:T(8,128)(2,1)} %own_ref.1) | copy-start | bytes 786436
  3.4 13.5 %collective-permute-start.1 = (bf16[64,4096]{1,0:T(8,128)(2,1)}, bf16[64,4096]{1,0:T(8,128)(2,1)}, u32[]{:S(2)}, u32[]{:S(2)}) collective-permute-start(bf16[64,4096]{1,0:T(8,128)(2,1)} %constant_dynamic-slice_fusion), channel_id=1, source_target_pairs={{0,2},{1,7},{2,4},{3,1},{4,6},{5,3},{6,0},{7,5},{8,10},{9,15},{10,... | collective-permute-start | bytes 1572872 | tf_op jit(solution)/shard_map/ppermute | solution.py:31
  5.9 12.8 %collective-permute-start.4 = (bf16[64,4096]{1,0:T(8,128)(2,1)}, bf16[64,4096]{1,0:T(8,128)(2,1)}, u32[]{:S(2)}, u32[]{:S(2)}) collective-permute-start(bf16[64,4096]{1,0:T(8,128)(2,1)} %constant_dynamic-slice_fusion), channel_id=1, source_target_pairs={{0,7},{1,2},{2,1},{3,4},{4,3},{5,6},{6,5},{7,0},{8,15},{9,10},{10,... | collective-permute-start | bytes 1572872 | tf_op jit(solution)/shard_map/ppermute | solution.py:31
  8.1 0.7 copy-start.3
  10.7 22.5 %copy-start = (bf16[256,4096]{1,0:T(8,128)(2,1)S(1)}, bf16[256,4096]{1,0:T(8,128)(2,1)}, u32[]{:S(2)}) copy-start(bf16[256,4096]{1,0:T(8,128)(2,1)} %refs_0_.1) | copy-start | bytes 6291460
  10.7 22.5 %copy-start.1 = (bf16[4096,128]{1,0:T(8,128)(2,1)S(1)}, bf16[4096,128]{1,0:T(8,128)(2,1)}, u32[]{:S(2)}) copy-start(bf16[4096,128]{1,0:T(8,128)(2,1)} %refs_7_.3) | copy-start | bytes 3145732
  20.6 25.3 %collective-permute-start.5 = (bf16[128,4096]{1,0:T(8,128)(2,1)}, bf16[128,4096]{1,0:T(8,128)(2,1)}, u32[]{:S(2)}, u32[]{:S(2)}) collective-permute-start(bf16[128,4096]{1,0:T(8,128)(2,1)} %constant_dynamic-update-slice_fusion.refs_0_), channel_id=1, source_target_pairs={{0,32},{1,97},{2,34},{3,99},{4,36},{5,101},{6,38},{7,103},{8,40},{... | collective-permute-start | bytes 3145736 | tf_op jit(solution)/shard_map/ppermute | solution.py:31
  23.3 22.6 %collective-permute-start.6 = (bf16[128,4096]{1,0:T(8,128)(2,1)}, bf16[128,4096]{1,0:T(8,128)(2,1)}, u32[]{:S(2)}, u32[]{:S(2)}) collective-permute-start(bf16[128,4096]{1,0:T(8,128)(2,1)} %constant_dynamic-update-slice_fusion.refs_0_), channel_id=1, source_target_pairs={{0,8},{1,25},{2,10},{3,27},{4,12},{5,29},{6,14},{7,31},{8,16},{9,1... | collective-permute-start | bytes 3145736 | tf_op jit(solution)/shard_map/ppermute | solution.py:31
  27.7 18.2 %collective-permute-start.3 = (bf16[64,4096]{1,0:T(8,128)(2,1)}, bf16[64,4096]{1,0:T(8,128)(2,1)S(1)}, u32[]{:S(2)}, u32[]{:S(2)}) collective-permute-start(bf16[64,4096]{1,0:T(8,128)(2,1)} %collective-permute-done.1), channel_id=1, source_target_pairs={{0,2},{1,7},{2,4},{3,1},{4,6},{5,3},{6,0},{7,5},{8,10},{9,15},{10,... | collective-permute-start | bytes 1572872 | tf_op jit(solution)/shard_map/ppermute | solution.py:31
  30.8 12.1 %collective-permute-start.7 = (bf16[64,4096]{1,0:T(8,128)(2,1)}, bf16[64,4096]{1,0:T(8,128)(2,1)S(1)}, u32[]{:S(2)}, u32[]{:S(2)}) collective-permute-start(bf16[64,4096]{1,0:T(8,128)(2,1)} %constant_dynamic-slice_fusion.1), channel_id=1, source_target_pairs={{0,2},{1,7},{2,4},{3,1},{4,6},{5,3},{6,0},{7,5},{8,10},{9,15},{10,... | collective-permute-start | bytes 1572872 | tf_op jit(solution)/shard_map/ppermute | solution.py:31
  31.0 1.0 copy-start.4
  31.9 1.3 %copy-start.5 = (bf16[1024,128]{1,0:T(8,128)(2,1)S(1)}, bf16[1024,128]{1,0:T(8,128)(2,1)}, u32[]{:S(2)}) copy-start(bf16[1024,128]{1,0:T(8,128)(2,1)} %copy-done.3) | copy-start | bytes 786436
  42.9 22.1 %collective-permute-start.10 = (bf16[64,4096]{1,0:T(8,128)(2,1)S(1)}, bf16[64,4096]{1,0:T(8,128)(2,1)S(1)}, u32[]{:S(2)}, u32[]{:S(2)}) collective-permute-start(bf16[64,4096]{1,0:T(8,128)(2,1)S(1)} %collective-permute-done.7.refs_4_), channel_id=1, source_target_pairs={{0,2},{1,7},{2,4},{3,1},{4,6},{5,3},{6,0},{7,5},{8,10},{9,15},{10,... | collective-permute-start | bytes 1572872 | tf_op jit(solution)/shard_map/ppermute | solution.py:31
  48.0 17.0 %collective-permute-start.8 = (bf16[96,4096]{1,0:T(8,128)(2,1)S(1)}, bf16[96,4096]{1,0:T(8,128)(2,1)S(1)}, u32[]{:S(2)}, u32[]{:S(2)}) collective-permute-start(bf16[96,4096]{1,0:T(8,128)(2,1)S(1)} %get-tuple-element.56), channel_id=1, source_target_pairs={{0,32},{1,97},{2,34},{3,99},{4,36},{5,101},{6,38},{7,103},{8,40},{... | collective-permute-start | bytes 2359304 | tf_op jit(solution)/shard_map/ppermute | solution.py:31
  48.6 16.5 %collective-permute-start.9 = (bf16[96,4096]{1,0:T(8,128)(2,1)S(1)}, bf16[96,4096]{1,0:T(8,128)(2,1)S(1)}, u32[]{:S(2)}, u32[]{:S(2)}) collective-permute-start(bf16[96,4096]{1,0:T(8,128)(2,1)S(1)} %get-tuple-element.55), channel_id=1, source_target_pairs={{0,8},{1,25},{2,10},{3,27},{4,12},{5,29},{6,14},{7,31},{8,16},{9,1... | collective-permute-start | bytes 2359304 | tf_op jit(solution)/shard_map/ppermute | solution.py:31
  74.5 9.8 %copy-start.6 = (s32[2048]{0:T(1024)S(1)}, s32[2048]{0:T(1024)}, u32[]{:S(2)}) copy-start(s32[2048]{0:T(1024)} %param.12) | copy-start | bytes 24580
  76.3 23.3 %all-to-all-start = ((bf16[128,24,128]{2,1,0:T(8,128)(2,1)}), bf16[128,24,128]{2,1,0:T(8,128)(2,1)S(1)}, u32[]{:S(2)}, u32[]{:S(2)}) async-start(bf16[128,24,128]{2,1,0:T(8,128)(2,1)} %get-tuple-element.47), calls=%async_computation | async-start | bytes 1572864 | tf_op jit(solution)/shard_map/all_to_all | solution.py:410
  83.1 21.9 %collective-permute-start.11 = (f32[8,4,32,128]{3,2,1,0:T(8,128)S(1)}, f32[8,4,32,128]{3,2,1,0:T(8,128)S(1)}, u32[]{:S(2)}, u32[]{:S(2)}) collective-permute-start(f32[8,4,32,128]{3,2,1,0:T(8,128)S(1)} %get-tuple-element.48.own_ref), channel_id=1, source_target_pairs={{0,1},{1,0},{2,3},{3,2},{4,5},{5,4},{6,7},{7,6},{8,9},{9,8},{10,11... | collective-permute-start | bytes 1572872 | tf_op jit(solution)/shard_map/ppermute | solution.py:31
  101.1 10.3 %all-to-all-start.1 = ((f32[16,8,256]{2,1,0:T(8,128)}), f32[16,8,256]{2,1,0:T(8,128)S(1)}, u32[]{:S(2)}, u32[]{:S(2)}) async-start(f32[16,8,256]{2,1,0:T(8,128)} %shard_map.78), calls=%async_computation.1 | async-start | bytes 262144 | tf_op jit(solution)/shard_map/all_to_all | solution.py:411

commit v3 on v2

--- a/solution.py
+++ b/solution.py
@@ -11,7 +11,7 @@
 SEQS = 16
 ALL = ("y", "z", "x", "c")
 TILE = 256
-LIMIT = 44 * 1024 * 1024
+LIMIT = 26 * 1024 * 1024
 BF = jnp.bfloat16
 F32 = jnp.float32
 
@@ -51,48 +51,80 @@
     return (y, z, x, 1 - c)
 
 
-def flash_kernel(sizes, bounds, *refs):
+def rows_kernel(plan, count, *refs):
+    where, refs = refs[0], refs[1:]
+    sources, results, sems = refs[:count], refs[count:-1], refs[-1]
+    copies = []
+    for n, (source, start, rows, to, at) in enumerate(plan):
+        if isinstance(start, tuple):
+            start = pl.multiple_of(where[start[0]] * rows, rows)
+        copies.append(
+            pltpu.make_async_copy(
+                sources[source].at[pl.ds(start, rows), :],
+                results[to].at[at : at + rows, :],
+                sems.at[n],
+            )
+        )
+    for copy in copies:
+        copy.start()
+    for copy in copies:
+        copy.wait()
+
+
+def rows_of(plan, where, sources, lengths, limit):
+    away = pl.BlockSpec(memory_space=pl.ANY)
+    width = sources[0].shape[1]
+    return pl.pallas_call(
+        functools.partial(rows_kernel, plan, len(sources)),
+        in_specs=[pl.BlockSpec(memory_space=pltpu.SMEM)] + [away] * len(sources),
+        out_specs=[pl.BlockSpec(memory_space=pl.ANY)] * len(lengths),
+        out_shape=[jax.ShapeDtypeStruct((n, width), BF) for n in lengths],
+        scratch_shapes=[pltpu.SemaphoreType.DMA((len(plan),))],
+        compiler_params=pltpu.CompilerParams(vmem_limit_bytes=limit),
+        cost_estimate=pl.CostEstimate(
+            flops=0, bytes_accessed=4 * width * sum(lengths), transcendentals=0
+        ),
+    )(where, *sources)
+
+
+def flash_kernel(sizes, *refs):
     count = len(sizes)
     pieces, heads = refs[:count], refs[count : count + 2]
-    proj_refs, in_ref = refs[count + 2 : count + 4], refs[count + 4]
+    projs, in_ref = refs[count + 2 : count + 4], refs[count + 4]
     out_ref, lse_ref, side_ref = refs[count + 5 : count + 8]
-    tok, held, proj, in_proj, scores, piece_sem, head_sem, proj_sem = refs[count + 8 :]
+    tok, held, scores, sems, head_sem = refs[count + 8 :]
     rows = heads[0].shape[0]
-
-    arrivals = []
+    chunk = 512
+
+    copies = []
     at = 0
     for number, (size, piece) in enumerate(zip(sizes, pieces)):
-        arrivals.append(
-            pltpu.make_async_copy(piece, tok.at[at : at + size, :], piece_sem.at[number])
-        )
+        copies.append(pltpu.make_async_copy(piece, tok.at[at : at + size, :], sems.at[number]))
         at += size
-    blocks = []
-    for number, (low, high) in enumerate(zip(bounds, bounds[1:])):
-        head, shift = (heads[0], 0) if low < rows else (heads[1], rows)
-        blocks.append(
-            pltpu.make_async_copy(
-                head.at[low - shift : high - shift, :], held.at[low:high, :], head_sem.at[number]
-            )
-        )
-    others = [
-        pltpu.make_async_copy(proj_refs[0], proj.at[0:rows, :], proj_sem.at[0]),
-        pltpu.make_async_copy(proj_refs[1], proj.at[rows : 2 * rows, :], proj_sem.at[1]),
-        pltpu.make_async_copy(in_ref, in_proj, proj_sem.at[2]),
+    blocks = [
+        pltpu.make_async_copy(
+            heads[1].at[low : low + chunk, :], held.at[low : low + chunk, :], head_sem.at[n]
+        )
+        for n, low in enumerate(range(0, rows, chunk))
     ]
-    for copy in arrivals + blocks + others:
+    for copy in copies + blocks:
         copy.start()
-    for copy in arrivals:
+    for copy in copies:
         copy.wait()
 
+    tile = 1024 if tok.shape[0] <= 256 else 512
     dims = (((1,), (1,)), ((), ()))
-    for block, low, high in zip(blocks, bounds, bounds[1:]):
+    for low in range(0, rows, tile):
+        scores[:, low : low + tile] = lax.dot_general(
+            tok[...], heads[0][low : low + tile, :], dims, preferred_element_type=F32
+        )
+    for block in blocks:
         block.wait()
-        scores[:, low:high] = lax.dot_general(
-            tok[...], held[low:high, :], dims, preferred_element_type=F32
-        )
-    for copy in others:
-        copy.wait()
-    side_ref[...] = jnp.dot(tok[...], in_proj[...], preferred_element_type=F32)
+    for low in range(0, rows, tile):
+        scores[:, rows + low : rows + low + tile] = lax.dot_general(
+            tok[...], held[low : low + tile, :], dims, preferred_element_type=F32
+        )
+    side_ref[...] = jnp.dot(tok[...], in_ref[...], preferred_element_type=F32)
 
     step = 512
     best = scores[:, 0:step]
@@ -104,9 +136,8 @@
     for low in range(0, 2 * rows, step):
         power = jnp.exp(scores[:, low : low + step] - best)
         total = power if low == 0 else total + power
-        part = jnp.dot(
-            power.astype(BF), proj[low : low + step, :], preferred_element_type=F32
-        )
+        proj = projs[low // rows][low % rows : low % rows + step, :]
+        part = jnp.dot(power.astype(BF), proj, preferred_element_type=F32)
         mixed = part if low == 0 else mixed + part
     total = jnp.sum(total, axis=1, keepdims=True)
     out_ref[...] = mixed / total
@@ -118,27 +149,23 @@
     n = sum(sizes)
     rows, depth = own.shape
     rank = proj_own.shape[1]
-    bounds = (0, 256, 512, 1024, 1536, 2048)
     here = pl.BlockSpec(memory_space=pltpu.VMEM)
     away = pl.BlockSpec(memory_space=pl.ANY)
     return pl.pallas_call(
-        functools.partial(flash_kernel, sizes, bounds),
-        in_specs=[away] * (len(pieces) + 5),
+        functools.partial(flash_kernel, sizes),
+        in_specs=[away] * len(pieces) + [here, away, here, here, here],
         out_specs=[here] * 3,
         out_shape=[jax.ShapeDtypeStruct((n, rank), F32)] * 3,
         scratch_shapes=[
             pltpu.VMEM((n, depth), BF),
-            pltpu.VMEM((2 * rows, depth), BF),
-            pltpu.VMEM((2 * rows, rank), BF),
-            pltpu.VMEM(in_proj.shape, BF),
+            pltpu.VMEM((rows, depth), BF),
             pltpu.VMEM((n, 2 * rows), F32),
             pltpu.SemaphoreType.DMA((len(pieces),)),
-            pltpu.SemaphoreType.DMA((len(bounds) - 1,)),
-            pltpu.SemaphoreType.DMA((3,)),
+            pltpu.SemaphoreType.DMA((2,)),
         ],
         compiler_params=pltpu.CompilerParams(vmem_limit_bytes=LIMIT),
         cost_estimate=pl.CostEstimate(
-            flops=2 * n * 2 * rows * depth, bytes_accessed=2 * rows * depth * 2, transcendentals=0
+            flops=2 * n * 2 * rows * depth, bytes_accessed=n * depth * 2, transcendentals=0
         ),
     )(*pieces, own, sib, proj_own, proj_sib, in_proj)
 
@@ -331,24 +358,8 @@
         out_specs=here,
         out_shape=jax.ShapeDtypeStruct((8, SEQS, store.shape[0] // 8), F32),
         scratch_shapes=[pltpu.VMEM(store.shape, BF), pltpu.SemaphoreType.DMA((8,))],
-        compiler_params=pltpu.CompilerParams(vmem_limit_bytes=50 * 1024 * 1024),
+        compiler_params=pltpu.CompilerParams(vmem_limit_bytes=48 * 1024 * 1024),
     )(flags, out, own, sib, seq, store)
-
-
-def finish_kernel(got_ref, out_ref):
-    total = got_ref[0]
-    for source in range(1, 8):
-        total = total + got_ref[source]
-    out_ref[...] = total
-
-
-def finish(got):
-    return pl.pallas_call(
-        finish_kernel,
-        in_specs=[pl.BlockSpec(memory_space=pltpu.VMEM)],
-        out_specs=pl.BlockSpec(memory_space=pltpu.VMEM),
-        out_shape=jax.ShapeDtypeStruct((SEQS, 256), F32),
-    )(got)
 
 
 def by_place(per_token):
@@ -362,25 +373,34 @@
     sign = 1 - 2 * c
     rows = out_head.shape[0]
 
-    mine = lax.dynamic_slice_in_dim(hidden, k * 64, 64, 0)
-
+    quarters = jnp.stack([k, 3 - k]).astype(jnp.int32)
+
+    mine, mine_d = rows_of(
+        ((0, (0,), 64, 0, 0), (0, (1,), 64, 1, 0)), quarters, [hidden], [64, 64], 60 << 20
+    )
     near_a = move(mine, along_x)
     near_b = move(mine, along_x_crossed)
     head_sib = move(out_head, to_sibling)
     proj_sib = move(out_proj, to_sibling)
-    again, proj_sib = lax.optimization_barrier((hidden, proj_sib))
-    mine_d = lax.dynamic_slice_in_dim(again, (3 - k) * 64, 64, 0)
     mine_d, near_a, head_sib = lax.optimization_barrier((mine_d, near_a, head_sib))
     far_k = move(near_a, along_x)
     near_a_d = move(mine_d, along_x)
-    near = jnp.concatenate([near_a, near_b], axis=0)
+    near = rows_of(((0, 0, 64, 0, 0), (1, 0, 64, 0, 64)), quarters, [near_a, near_b], [128], 16 << 20)[0]
     near_y = move(near, along_y)
     near_z = move(near, along_z)
+
     rest = (out_head, head_sib, out_proj, proj_sib, in_proj)
     first = flash([hidden], *rest)
     first, far_k, near_y, near_z = lax.optimization_barrier((first, far_k, near_y, near_z))
-    last_y = move(jnp.concatenate([far_k, near_z[64:96]], axis=0), along_y)
-    last_z = move(jnp.concatenate([far_k, near_y[96:128]], axis=0), along_z)
+    last_y, last_z = rows_of(
+        ((0, 0, 64, 0, 0), (2, 64, 32, 0, 64), (0, 0, 64, 1, 0), (1, 96, 32, 1, 64)),
+        quarters,
+        [far_k, near_y, near_z],
+        [96, 96],
+        16 << 20,
+    )
+    last_y = move(last_y, along_y)
+    last_z = move(last_z, along_z)
     far_d = move(near_a_d, along_x)
 
     first_row = lax.axis_index(ALL) * rows
@@ -407,10 +427,12 @@
     ).astype(jnp.int32)
     send, side = pack(place, (first, second, third), hot)
     side_sib = move(side, to_sibling)
+
     got = lax.all_to_all(send, ALL, 0, 0, tiled=True)
+
     out = lax.all_to_all(merge(got), ("y", "z"), 0, 0, tiled=True)
     partial = score(kinds.astype(jnp.int32), out, side, side_sib, seq_table, grad_store)
-    return finish(lax.all_to_all(partial, ("x", "c"), 0, 0, tiled=True)).T
+    return jnp.sum(lax.all_to_all(partial, ("x", "c"), 0, 0, tiled=True), axis=0).T
 
 
 def solution(mesh):

time: 132 us -> 157 us (1.19)
  Pallas kernels: 49.1 us -> 74.5 us
  waiting for transfers between devices: 29 us -> 31.7 us
  starting transfers between devices: 29.4 us -> 27.1 us
    pallas_call x4 -> x6, Pallas kernels: 36.7 us -> 62.1 us  [the longest x3 34.9 us: rows_of(): pl.pallas_call(functools.partial(rows_kernel, plan, len(sources)), in_spe...]
    unnamed x15 -> x28, local copies, waits for them, and re-layouts: 3.56 us -> 9.84 us
    dynamic_slice x2 -> x0, local copies, waits for them, and re-layouts: 3.82 us -> none  [the longest x1 1.95 us: on_device(): mine = lax.dynamic_slice_in_dim(hidden, k * 64, 64, 0)]
    ppermute x12, waiting for transfers between devices: 7.26 us -> 9.96 us  [move(): return lax.ppermute(value, ALL, pairs)]
    ppermute x12, starting transfers between devices: 19.1 us -> 17 us  [move(): return lax.ppermute(value, ALL, pairs)]
    slice x2 -> x0, local copies, waits for them, and re-layouts: 1.94 us -> none  [the longest x1 0.97 us: on_device(): last_z = move(jnp.concatenate([far_k, near_y[96:128]], axis=0), along_z)]
    concatenate x1 -> x0, local copies, waits for them, and re-layouts: 1.86 us -> none  [on_device(): near = jnp.concatenate([near_a, near_b], axis=0)]
  transfers between devices with their start and end apart: 14 -> 14, of which waited for: 5 -> 4; matrix products, arithmetic and copies ran while one was open for 7% -> 2% of each run, Pallas kernels for 22% -> 37%
where the time goes in v3:
time: 157 us; the launch traced here: 156 us
  Pallas kernels  74.5 us (47%)
  waiting for transfers between devices  31.7 us (20%)
  starting transfers between devices  27.1 us (17%)
  local copies, waits for them, and re-layouts  11.4 us (7%)
  blocking collectives  9.51 us (6%)
    pallas_call x3, Pallas kernels, rows_of(): pl.pallas_call(functools.partial(rows_kernel, plan, len(sources)), in_spe...  34.9 us
    pallas_call x3, Pallas kernels, flash(): pl.pallas_call(functools.partial(flash_kernel, sizes), in_specs=[away] *...  27.2 us
    ppermute x12, starting transfers between devices, move(): return lax.ppermute(value, ALL, pairs)  17 us
    all_to_all x1, waiting for transfers between devices, on_device(): got = lax.all_to_all(send, ALL, 0, 0, tiled=True)  15.3 us
    ppermute x12, waiting for transfers between devices, move(): return lax.ppermute(value, ALL, pairs)  9.96 us
    unnamed x28, local copies, waits for them, and re-layouts  9.84 us
    all_to_all x1, blocking collectives, on_device(): lax.all_to_all(partial, ('x', 'c'), 0, 0, tiled=True)  9.51 us
    pallas_call x1, Pallas kernels, score(): pl.pallas_call(score_kernel, in_specs=[pl.BlockSpec(memory_space=pltpu.SM...  7.88 us
  transfers between devices with their start and end apart: 14, of which 4 were waited for; matrix products, arithmetic and copies ran while one was open for 2% of the time, Pallas kernels for 37%

profile of v3, /device:TPU:1, one launch (start us, length us, event | category | flops | bytes accessed | tf_op | source)
XLA Modules:
  0.0 155.9 jit_solution(4335905085666254505)
XLA Ops:
  0.0 1.4 collective-permute-start.1
  2.1 33.5 %shard_map.73 = (bf16[64,4096]{1,0:T(8,128)(2,1)}, bf16[64,4096]{1,0:T(8,128)(2,1)}) custom-call(s32[2]{0:T(128)} %pad_add_fusion.refs_0_, bf16[256,4096]{1,0:T(8,128)(2,1)} %refs_0_.1), custom_call_target="tpu_custom_call" | custom-call | bytes 2097152 | tf_op jit(solution)/shard_map/pallas_call | solution.py:77
  35.6 2.6 %collective-permute-start = (bf16[64,4096]{1,0:T(8,128)(2,1)}, bf16[64,4096]{1,0:T(8,128)(2,1)S(1)}, u32[]{:S(2)}, u32[]{:S(2)}) collective-permute-start(bf16[64,4096]{1,0:T(8,128)(2,1)} %get-tuple-element.30), channel_id=1, source_target_pairs={{0,2},{1,7},{2,4},{3,1},{4,6},{5,3},{6,0},{7,5},{8,10},{9,15},{10,... | collective-permute-start | bytes 1572872 | tf_op jit(solution)/shard_map/ppermute | solution.py:31
  39.9 9.3 %collective-permute-done.refs_1_ = bf16[64,4096]{1,0:T(8,128)(2,1)S(1)} collective-permute-done((bf16[64,4096]{1,0:T(8,128)(2,1)}, bf16[64,4096]{1,0:T(8,128)(2,1)S(1)}, u32[]{:S(2)}, u32[]{:S(2)}) %collective-permute-start) | collective-permute-done | bytes 524320 | tf_op jit(solution)/shard_map/ppermute | solution.py:31
  51.2 2.9 %collective-permute-start.5 = (bf16[128,4096]{1,0:T(8,128)(2,1)S(1)}, bf16[128,4096]{1,0:T(8,128)(2,1)S(1)}, u32[]{:S(2)}, u32[]{:S(2)}) collective-permute-start(bf16[128,4096]{1,0:T(8,128)(2,1)S(1)} %shard_map.75.refs_0_), channel_id=1, source_target_pairs={{0,32},{1,97},{2,34},{3,99},{4,36},{5,101},{6,38},{7,103},{8,40},{... | collective-permute-start | bytes 3145736 | tf_op jit(solution)/shard_map/ppermute | solution.py:31
  54.1 3.8 %collective-permute-start.6 = (bf16[128,4096]{1,0:T(8,128)(2,1)S(1)}, bf16[128,4096]{1,0:T(8,128)(2,1)S(1)}, u32[]{:S(2)}, u32[]{:S(2)}) collective-permute-start(bf16[128,4096]{1,0:T(8,128)(2,1)S(1)} %shard_map.75.refs_0_), channel_id=1, source_target_pairs={{0,8},{1,25},{2,10},{3,27},{4,12},{5,29},{6,14},{7,31},{8,16},{9,1... | collective-permute-start | bytes 3145736 | tf_op jit(solution)/shard_map/ppermute | solution.py:31
  58.4 3.4 %collective-permute-start.3 = (bf16[64,4096]{1,0:T(8,128)(2,1)}, bf16[64,4096]{1,0:T(8,128)(2,1)S(1)}, u32[]{:S(2)}, u32[]{:S(2)}) collective-permute-start(bf16[64,4096]{1,0:T(8,128)(2,1)} %copy-done.8), channel_id=1, source_target_pairs={{0,2},{1,7},{2,4},{3,1},{4,6},{5,3},{6,0},{7,5},{8,10},{9,15},{10,... | collective-permute-start | bytes 1572872 | tf_op jit(solution)/shard_map/ppermute | solution.py:31
  62.9 1.3 shard_map.79.refs_9_
  64.2 3.4 %copy-done = bf16[1024,4096]{1,0:T(8,128)(2,1)S(1)} copy-done((bf16[1024,4096]{1,0:T(8,128)(2,1)S(1)}, bf16[1024,4096]{1,0:T(8,128)(2,1)}, u32[]{:S(2)}) %copy-start) | copy-done | bytes 8388632
  67.6 1.6 %copy-done.2 = bf16[256,4096]{1,0:T(8,128)(2,1)S(1)} copy-done((bf16[256,4096]{1,0:T(8,128)(2,1)S(1)}, bf16[256,4096]{1,0:T(8,128)(2,1)}, u32[]{:S(2)}) %copy-start.2) | copy-done | bytes 2097176
  69.2 1.2 copy-done.3
  71.4 7.3 %shard_map.74 = (f32[256,128]{1,0:T(8,128)S(1)}, f32[256,128]{1,0:T(8,128)S(1)}, f32[256,128]{1,0:T(8,128)S(1)}) custom-call(bf16[256,4096]{1,0:T(8,128)(2,1)S(1)} %copy-done.2, bf16[1024,4096]{1,0:T(8,128)(2,1)S(1)} %copy-done, bf16[1024,4096]{1,0:T(8,128)(2,1)} %collective-permute-done.1.refs_2_.refs_6_.refs_4_, bf16[1024,128]{1,0:T(8,128)(2,1)S(1)} %copy-done.6, ...), custom_call_target="tpu_custom_call" | custom-call | flops 4294967296 | bytes 2097152 | tf_op jit(solution)/shard_map/pallas_call | solution.py:154
  80.2 12.7 %shard_map.76 = (f32[512,128]{1,0:T(8,128)S(1)}, f32[512,128]{1,0:T(8,128)S(1)}, f32[512,128]{1,0:T(8,128)S(1)}) custom-call(bf16[128,4096]{1,0:T(8,128)(2,1)S(1)} %shard_map.75.refs_0_, bf16[128,4096]{1,0:T(8,128)(2,1)S(1)} %collective-permute-done.5.refs_1_.refs_2_, bf16[128,4096]{1,0:T(8,128)(2,1)S(1)} %collective-permute-done.6.refs_2_.refs_3_, ...), custom_call_target="tpu_custom_call" | custom-call | flops 8589934592 | bytes 4194304 | tf_op jit(solution)/shard_map/pallas_call | solution.py:154
  92.9 7.3 %shard_map.78 = (f32[256,128]{1,0:T(8,128)S(1)}, f32[256,128]{1,0:T(8,128)S(1)}, f32[256,128]{1,0:T(8,128)S(1)}) custom-call(bf16[96,4096]{1,0:T(8,128)(2,1)S(1)} %collective-permute-done.8.refs_0_, bf16[96,4096]{1,0:T(8,128)(2,1)S(1)} %collective-permute-done.9.refs_1_, bf16[64,4096]{1,0:T(8,128)(2,1)S(1)} %collective-permute-done.10.refs_2_, ...), custom_call_target="tpu_custom_call" | custom-call | flops 4294967296 | bytes 2097152 | tf_op jit(solution)/shard_map/pallas_call | solution.py:154
  100.2 1.8 %shard_map.80 = (bf16[128,24,128]{2,1,0:T(8,128)(2,1)}, f32[8,4,32,128]{3,2,1,0:T(8,128)S(1)}) custom-call(s32[5]{0:T(128)S(1)} %stack.45.place, f32[256,128]{1,0:T(8,128)S(1)} %get-tuple-element.36.refs_0_, f32[512,128]{1,0:T(8,128)S(1)} %get-tuple-element.41.refs_1_, f32[256,128]{1,0:T(8,128)S(1)} %get-tuple-element.44.refs_2_, ...), custom_call_target="tpu_custom_call" | custom-call | tf_op jit(solution)/shard_map/pallas_call | solution.py:249
  102.0 6.6 %all-to-all-start = ((bf16[128,24,128]{2,1,0:T(8,128)(2,1)}), bf16[128,24,128]{2,1,0:T(8,128)(2,1)S(1)}, u32[]{:S(2)}, u32[]{:S(2)}) async-start(bf16[128,24,128]{2,1,0:T(8,128)(2,1)} %get-tuple-element.51), calls=%async_computation | async-start | bytes 1572864 | tf_op jit(solution)/shard_map/all_to_all | solution.py:431
  108.6 1.1 collective-permute-start.11
  109.8 15.3 %all-to-all-done.got_ref = bf16[128,24,128]{2,1,0:T(8,128)(2,1)S(1)} async-done(((bf16[128,24,128]{2,1,0:T(8,128)(2,1)}), bf16[128,24,128]{2,1,0:T(8,128)(2,1)S(1)}, u32[]{:S(2)}, u32[]{:S(2)}) %all-to-all-start) | async-done | bytes 786464 | tf_op jit(solution)/shard_map/all_to_all | solution.py:431
  125.1 1.4 shard_map.81
  126.6 3.5 %all-to-all-start.1 = ((f32[16,8,256]{2,1,0:T(8,128)}), f32[16,8,256]{2,1,0:T(8,128)S(1)}, u32[]{:S(2)}, u32[]{:S(2)}) async-start(f32[16,8,256]{2,1,0:T(8,128)} %shard_map.81), calls=%async_computation.1 | async-start | bytes 262144 | tf_op jit(solution)/shard_map/all_to_all | solution.py:433
  130.5 6.4 %all-to-all-done.1.out_ref = f32[16,8,256]{2,1,0:T(8,128)S(1)} async-done(((f32[16,8,256]{2,1,0:T(8,128)}), f32[16,8,256]{2,1,0:T(8,128)S(1)}, u32[]{:S(2)}, u32[]{:S(2)}) %all-to-all-start.1) | async-done | bytes 131104 | tf_op jit(solution)/shard_map/all_to_all | solution.py:433
  136.9 1.0 copy-done.10
  137.9 7.9 %shard_map.82 = f32[8,16,256]{2,1,0:T(8,128)S(1)} custom-call(s32[4]{0:T(128)S(1)} %get-tuple-element.58.flags, f32[16,8,256]{2,1,0:T(8,128)S(1)} %all-to-all-done.1.out_ref, f32[8,4,32,128]{3,2,1,0:T(8,128)S(1)} %copy-done.10, f32[8,4,32,128]{3,2,1,0:T(8,128)S(1)} %collective-permute-done.11.sib_ref, s32[8,256]{1,0:T(8,128)S(1)} %reshape.46.seq_ref, ...), custom_call_target="tpu_custom_call" | custom-call | tf_op jit(solution)/shard_map/pallas_call | solution.py:348
  145.8 9.5 %all_to_all.15 = f32[8,16,256]{2,1,0:T(8,128)S(1)} all-to-all(f32[8,16,256]{2,1,0:T(8,128)S(1)} %shard_map.82), channel_id=1, replica_groups=mesh['y'=4,'z'=4,'x'=4,'c'=2] {'x','c'}, dimensions={0} | all-to-all | bytes 262144 | tf_op jit(solution)/shard_map/all_to_all | solution.py:435
  (66 shorter events, 9.4 us)
Async XLA Ops:
  0.0 49.2 %collective-permute-start.1 = (bf16[1024,4096]{1,0:T(8,128)(2,1)}, bf16[1024,4096]{1,0:T(8,128)(2,1)}, u32[]{:S(2)}, u32[]{:S(2)}) collective-permute-start(bf16[1024,4096]{1,0:T(8,128)(2,1)} %refs_3_.3), channel_id=1, source_target_pairs={{0,1},{1,0},{2,3},{3,2},{4,5},{5,4},{6,7},{7,6},{8,9},{9,8},{10,11... | collective-permute-start | bytes 25165832 | tf_op jit(solution)/shard_map/ppermute | solution.py:31
  35.6 13.5 %collective-permute-start = (bf16[64,4096]{1,0:T(8,128)(2,1)}, bf16[64,4096]{1,0:T(8,128)(2,1)S(1)}, u32[]{:S(2)}, u32[]{:S(2)}) collective-permute-start(bf16[64,4096]{1,0:T(8,128)(2,1)} %get-tuple-element.30), channel_id=1, source_target_pairs={{0,2},{1,7},{2,4},{3,1},{4,6},{5,3},{6,0},{7,5},{8,10},{9,15},{10,... | collective-permute-start | bytes 1572872 | tf_op jit(solution)/shard_map/ppermute | solution.py:31
  38.3 11.6 %collective-permute-start.4 = (bf16[64,4096]{1,0:T(8,128)(2,1)}, bf16[64,4096]{1,0:T(8,128)(2,1)S(1)}, u32[]{:S(2)}, u32[]{:S(2)}) collective-permute-start(bf16[64,4096]{1,0:T(8,128)(2,1)} %get-tuple-element.30), channel_id=1, source_target_pairs={{0,7},{1,2},{2,1},{3,4},{4,3},{5,6},{6,5},{7,0},{8,15},{9,10},{10,... | collective-permute-start | bytes 1572872 | tf_op jit(solution)/shard_map/ppermute | solution.py:31
  38.4 23.6 %collective-permute-start.2 = (bf16[1024,128]{1,0:T(8,128)(2,1)}, bf16[1024,128]{1,0:T(8,128)(2,1)S(1)}, u32[]{:S(2)}, u32[]{:S(2)}) collective-permute-start(bf16[1024,128]{1,0:T(8,128)(2,1)} %own_ref.1), channel_id=1, source_target_pairs={{0,1},{1,0},{2,3},{3,2},{4,5},{5,4},{6,7},{7,6},{8,9},{9,8},{10,11... | collective-permute-start | bytes 786440 | tf_op jit(solution)/shard_map/ppermute | solution.py:31
  49.2 2.0 %copy-start.8 = (bf16[64,4096]{1,0:T(8,128)(2,1)}, bf16[64,4096]{1,0:T(8,128)(2,1)S(1)}, u32[]{:S(2)}) copy-start(bf16[64,4096]{1,0:T(8,128)(2,1)S(1)} %collective-permute-done.refs_1_) | copy-start | bytes 1572868
  51.2 27.6 %collective-permute-start.5 = (bf16[128,4096]{1,0:T(8,128)(2,1)S(1)}, bf16[128,4096]{1,0:T(8,128)(2,1)S(1)}, u32[]{:S(2)}, u32[]{:S(2)}) collective-permute-start(bf16[128,4096]{1,0:T(8,128)(2,1)S(1)} %shard_map.75.refs_0_), channel_id=1, source_target_pairs={{0,32},{1,97},{2,34},{3,99},{4,36},{5,101},{6,38},{7,103},{8,40},{... | collective-permute-start | bytes 3145736 | tf_op jit(solution)/shard_map/ppermute | solution.py:31
  54.1 24.7 %collective-permute-start.6 = (bf16[128,4096]{1,0:T(8,128)(2,1)S(1)}, bf16[128,4096]{1,0:T(8,128)(2,1)S(1)}, u32[]{:S(2)}, u32[]{:S(2)}) collective-permute-start(bf16[128,4096]{1,0:T(8,128)(2,1)S(1)} %shard_map.75.refs_0_), channel_id=1, source_target_pairs={{0,8},{1,25},{2,10},{3,27},{4,12},{5,29},{6,14},{7,31},{8,16},{9,1... | collective-permute-start | bytes 3145736 | tf_op jit(solution)/shard_map/ppermute | solution.py:31
  58.4 20.3 %collective-permute-start.3 = (bf16[64,4096]{1,0:T(8,128)(2,1)}, bf16[64,4096]{1,0:T(8,128)(2,1)S(1)}, u32[]{:S(2)}, u32[]{:S(2)}) collective-permute-start(bf16[64,4096]{1,0:T(8,128)(2,1)} %copy-done.8), channel_id=1, source_target_pairs={{0,2},{1,7},{2,4},{3,1},{4,6},{5,3},{6,0},{7,5},{8,10},{9,15},{10,... | collective-permute-start | bytes 1572872 | tf_op jit(solution)/shard_map/ppermute | solution.py:31
  61.8 16.8 %collective-permute-start.7 = (bf16[64,4096]{1,0:T(8,128)(2,1)}, bf16[64,4096]{1,0:T(8,128)(2,1)S(1)}, u32[]{:S(2)}, u32[]{:S(2)}) collective-permute-start(bf16[64,4096]{1,0:T(8,128)(2,1)} %get-tuple-element.40), channel_id=1, source_target_pairs={{0,2},{1,7},{2,4},{3,1},{4,6},{5,3},{6,0},{7,5},{8,10},{9,15},{10,... | collective-permute-start | bytes 1572872 | tf_op jit(solution)/shard_map/ppermute | solution.py:31
  64.2 3.4 %copy-start = (bf16[1024,4096]{1,0:T(8,128)(2,1)S(1)}, bf16[1024,4096]{1,0:T(8,128)(2,1)}, u32[]{:S(2)}) copy-start(bf16[1024,4096]{1,0:T(8,128)(2,1)} %refs_3_.3) | copy-start | bytes 25165828
  67.6 1.6 %copy-start.2 = (bf16[256,4096]{1,0:T(8,128)(2,1)S(1)}, bf16[256,4096]{1,0:T(8,128)(2,1)}, u32[]{:S(2)}) copy-start(bf16[256,4096]{1,0:T(8,128)(2,1)} %refs_0_.1) | copy-start | bytes 6291460
  69.2 1.2 copy-start.3
  71.4 7.4 %copy-start.12 = (s32[2]{0:T(128)S(1)}, s32[2]{0:T(128)}, u32[]{:S(2)}) copy-start(s32[2]{0:T(128)} %pad_add_fusion.refs_0_) | copy-start | bytes 28
  71.4 8.8 %copy-start.1 = (bf16[1024,4096]{1,0:T(8,128)(2,1)S(1)}, bf16[1024,4096]{1,0:T(8,128)(2,1)}, u32[]{:S(2)}) copy-start(bf16[1024,4096]{1,0:T(8,128)(2,1)} %refs_3_.3) | copy-start | bytes 25165828
  71.4 8.8 %copy-start.4 = (bf16[4096,128]{1,0:T(8,128)(2,1)S(1)}, bf16[4096,128]{1,0:T(8,128)(2,1)}, u32[]{:S(2)}) copy-start(bf16[4096,128]{1,0:T(8,128)(2,1)} %refs_7_.3) | copy-start | bytes 3145732
  71.4 8.8 %copy-start.7 = (bf16[1024,128]{1,0:T(8,128)(2,1)S(1)}, bf16[1024,128]{1,0:T(8,128)(2,1)}, u32[]{:S(2)}) copy-start(bf16[1024,128]{1,0:T(8,128)(2,1)} %own_ref.1) | copy-start | bytes 786436
  78.7 14.2 %collective-permute-start.10 = (bf16[64,4096]{1,0:T(8,128)(2,1)S(1)}, bf16[64,4096]{1,0:T(8,128)(2,1)S(1)}, u32[]{:S(2)}, u32[]{:S(2)}) collective-permute-start(bf16[64,4096]{1,0:T(8,128)(2,1)S(1)} %collective-permute-done.7.refs_4_), channel_id=1, source_target_pairs={{0,2},{1,7},{2,4},{3,1},{4,6},{5,3},{6,0},{7,5},{8,10},{9,15},{10,... | collective-permute-start | bytes 1572872 | tf_op jit(solution)/shard_map/ppermute | solution.py:31
  79.5 13.4 %collective-permute-start.8 = (bf16[96,4096]{1,0:T(8,128)(2,1)S(1)}, bf16[96,4096]{1,0:T(8,128)(2,1)S(1)}, u32[]{:S(2)}, u32[]{:S(2)}) collective-permute-start(bf16[96,4096]{1,0:T(8,128)(2,1)S(1)} %get-tuple-element.42), channel_id=1, source_target_pairs={{0,32},{1,97},{2,34},{3,99},{4,36},{5,101},{6,38},{7,103},{8,40},{... | collective-permute-start | bytes 2359304 | tf_op jit(solution)/shard_map/ppermute | solution.py:31
  80.0 12.8 %collective-permute-start.9 = (bf16[96,4096]{1,0:T(8,128)(2,1)S(1)}, bf16[96,4096]{1,0:T(8,128)(2,1)S(1)}, u32[]{:S(2)}, u32[]{:S(2)}) collective-permute-start(bf16[96,4096]{1,0:T(8,128)(2,1)S(1)} %get-tuple-element.43), channel_id=1, source_target_pairs={{0,8},{1,25},{2,10},{3,27},{4,12},{5,29},{6,14},{7,31},{8,16},{9,1... | collective-permute-start | bytes 2359304 | tf_op jit(solution)/shard_map/ppermute | solution.py:31
  92.8 16.9 %copy-start.13 = (s32[2048]{0:T(1024)S(1)}, s32[2048]{0:T(1024)}, u32[]{:S(2)}) copy-start(s32[2048]{0:T(1024)} %param.12) | copy-start | bytes 24580
  102.0 34.9 %copy-start.9 = (f32[8,4,32,128]{3,2,1,0:T(8,128)}, f32[8,4,32,128]{3,2,1,0:T(8,128)S(1)}, u32[]{:S(2)}) copy-start(f32[8,4,32,128]{3,2,1,0:T(8,128)S(1)} %get-tuple-element.52.own_ref) | copy-start | bytes 1572868
  102.0 23.1 %all-to-all-start = ((bf16[128,24,128]{2,1,0:T(8,128)(2,1)}), bf16[128,24,128]{2,1,0:T(8,128)(2,1)S(1)}, u32[]{:S(2)}, u32[]{:S(2)}) async-start(bf16[128,24,128]{2,1,0:T(8,128)(2,1)} %get-tuple-element.51), calls=%async_computation | async-start | bytes 1572864 | tf_op jit(solution)/shard_map/all_to_all | solution.py:431
  108.6 21.9 %collective-permute-start.11 = (f32[8,4,32,128]{3,2,1,0:T(8,128)S(1)}, f32[8,4,32,128]{3,2,1,0:T(8,128)S(1)}, u32[]{:S(2)}, u32[]{:S(2)}) collective-permute-start(f32[8,4,32,128]{3,2,1,0:T(8,128)S(1)} %get-tuple-element.52.own_ref), channel_id=1, source_target_pairs={{0,1},{1,0},{2,3},{3,2},{4,5},{5,4},{6,7},{7,6},{8,9},{9,8},{10,11... | collective-permute-start | bytes 1572872 | tf_op jit(solution)/shard_map/ppermute | solution.py:31
  126.6 10.3 %all-to-all-start.1 = ((f32[16,8,256]{2,1,0:T(8,128)}), f32[16,8,256]{2,1,0:T(8,128)S(1)}, u32[]{:S(2)}, u32[]{:S(2)}) async-start(f32[16,8,256]{2,1,0:T(8,128)} %shard_map.81), calls=%async_computation.1 | async-start | bytes 262144 | tf_op jit(solution)/shard_map/all_to_all | solution.py:433
  (4 other events, 3.6 us)

commit v4 on v3

--- a/solution.py
+++ b/solution.py
@@ -71,13 +71,13 @@
         copy.wait()
 
 
-def rows_of(plan, where, sources, lengths, limit):
+def rows_of(plan, where, sources, lengths, limit, space=pl.ANY):
     away = pl.BlockSpec(memory_space=pl.ANY)
     width = sources[0].shape[1]
     return pl.pallas_call(
         functools.partial(rows_kernel, plan, len(sources)),
         in_specs=[pl.BlockSpec(memory_space=pltpu.SMEM)] + [away] * len(sources),
-        out_specs=[pl.BlockSpec(memory_space=pl.ANY)] * len(lengths),
+        out_specs=[pl.BlockSpec(memory_space=space)] * len(lengths),
         out_shape=[jax.ShapeDtypeStruct((n, width), BF) for n in lengths],
         scratch_shapes=[pltpu.SemaphoreType.DMA((len(plan),))],
         compiler_params=pltpu.CompilerParams(vmem_limit_bytes=limit),
@@ -87,12 +87,12 @@
     )(where, *sources)
 
 
-def flash_kernel(sizes, *refs):
+def flash_kernel(sizes, stream, *refs):
     count = len(sizes)
     pieces, heads = refs[:count], refs[count : count + 2]
     projs, in_ref = refs[count + 2 : count + 4], refs[count + 4]
     out_ref, lse_ref, side_ref = refs[count + 5 : count + 8]
-    tok, held, scores, sems, head_sem = refs[count + 8 :]
+    tok, held, scores, sems, head_sem = refs[count + 8 : count + 13]
     rows = heads[0].shape[0]
     chunk = 512
 
@@ -101,29 +101,52 @@
     for number, (size, piece) in enumerate(zip(sizes, pieces)):
         copies.append(pltpu.make_async_copy(piece, tok.at[at : at + size, :], sems.at[number]))
         at += size
-    blocks = [
-        pltpu.make_async_copy(
-            heads[1].at[low : low + chunk, :], held.at[low : low + chunk, :], head_sem.at[n]
-        )
-        for n, low in enumerate(range(0, rows, chunk))
-    ]
-    for copy in copies + blocks:
+    blocks = []
+    for head in heads if stream else heads[1:]:
+        for low in range(0, rows, chunk):
+            at = len(blocks)
+            blocks.append(
+                pltpu.make_async_copy(
+                    head.at[low : low + chunk, :],
+                    held.at[at * chunk : (at + 1) * chunk, :],
+                    head_sem.at[at],
+                )
+            )
+    others = []
+    if stream:
+        far = (*projs, in_ref)
+        *projs, in_ref = refs[count + 13 : count + 16]
+        for n, (source, target) in enumerate(zip(far, (*projs, in_ref))):
+            others.append(pltpu.make_async_copy(source, target, refs[count + 16].at[n]))
+    for copy in copies + blocks[:2] + others:
         copy.start()
     for copy in copies:
         copy.wait()
 
+    dims = (((1,), (1,)), ((), ()))
     tile = 1024 if tok.shape[0] <= 256 else 512
-    dims = (((1,), (1,)), ((), ()))
-    for low in range(0, rows, tile):
-        scores[:, low : low + tile] = lax.dot_general(
-            tok[...], heads[0][low : low + tile, :], dims, preferred_element_type=F32
-        )
-    for block in blocks:
-        block.wait()
-    for low in range(0, rows, tile):
-        scores[:, rows + low : rows + low + tile] = lax.dot_general(
-            tok[...], held[low : low + tile, :], dims, preferred_element_type=F32
-        )
+    if not stream:
+        for low in range(0, rows, tile):
+            scores[:, low : low + tile] = lax.dot_general(
+                tok[...], heads[0][low : low + tile, :], dims, preferred_element_type=F32
+            )
+        for block in blocks:
+            block.wait()
+        for low in range(0, rows, tile):
+            scores[:, rows + low : rows + low + tile] = lax.dot_general(
+                tok[...], held[low : low + tile, :], dims, preferred_element_type=F32
+            )
+    else:
+        for n, block in enumerate(blocks):
+            block.wait()
+            if n + 2 < len(blocks):
+                blocks[n + 2].start()
+            low = n * chunk
+            scores[:, low : low + chunk] = lax.dot_general(
+                tok[...], held[low : low + chunk, :], dims, preferred_element_type=F32
+            )
+    for copy in others:
+        copy.wait()
     side_ref[...] = jnp.dot(tok[...], in_ref[...], preferred_element_type=F32)
 
     step = 512
@@ -144,26 +167,31 @@
     lse_ref[...] = jnp.broadcast_to(best + jnp.log(total), lse_ref.shape)
 
 
-def flash(pieces, own, sib, proj_own, proj_sib, in_proj):
+def flash(pieces, own, sib, proj_own, proj_sib, in_proj, stream=False):
     sizes = tuple(p.shape[0] for p in pieces)
     n = sum(sizes)
     rows, depth = own.shape
     rank = proj_own.shape[1]
     here = pl.BlockSpec(memory_space=pltpu.VMEM)
     away = pl.BlockSpec(memory_space=pl.ANY)
+    extra = []
+    if stream:
+        extra = [pltpu.VMEM(a.shape, BF) for a in (proj_own, proj_sib, in_proj)]
+        extra.append(pltpu.SemaphoreType.DMA((3,)))
     return pl.pallas_call(
-        functools.partial(flash_kernel, sizes),
-        in_specs=[away] * len(pieces) + [here, away, here, here, here],
+        functools.partial(flash_kernel, sizes, stream),
+        in_specs=[away] * len(pieces) + ([away] * 5 if stream else [here, away, here, here, here]),
         out_specs=[here] * 3,
         out_shape=[jax.ShapeDtypeStruct((n, rank), F32)] * 3,
         scratch_shapes=[
             pltpu.VMEM((n, depth), BF),
-            pltpu.VMEM((rows, depth), BF),
+            pltpu.VMEM((2 * rows if stream else rows, depth), BF),
             pltpu.VMEM((n, 2 * rows), F32),
             pltpu.SemaphoreType.DMA((len(pieces),)),
-            pltpu.SemaphoreType.DMA((2,)),
-        ],
-        compiler_params=pltpu.CompilerParams(vmem_limit_bytes=LIMIT),
+            pltpu.SemaphoreType.DMA((4 if stream else 2,)),
+        ]
+        + extra,
+        compiler_params=pltpu.CompilerParams(vmem_limit_bytes=(44 << 20) if stream else LIMIT),
         cost_estimate=pl.CostEstimate(
             flops=2 * n * 2 * rows * depth, bytes_accessed=n * depth * 2, transcendentals=0
         ),
@@ -295,7 +323,9 @@
     )(got)
 
 
-def score_kernel(flags, out_ref, own_ref, sib_ref, seq_ref, store_ref, result_ref, store, sems):
+def score_kernel(
+    flags, out_ref, own_hbm, sib_hbm, seq_ref, store_ref, result_ref, own_ref, sib_ref, store, sems, side_sem
+):
     rows = store.shape[0] // 8
     copies = [
         pltpu.make_async_copy(
@@ -305,8 +335,14 @@
         )
         for n in range(8)
     ]
-    for copy in copies:
+    sides = [
+        pltpu.make_async_copy(own_hbm, own_ref, side_sem.at[0]),
+        pltpu.make_async_copy(sib_hbm, sib_ref, side_sem.at[1]),
+    ]
+    for copy in sides + copies[:3]:
         copy.start()
+    for copy in sides:
+        copy.wait()
     total = jnp.zeros((256, 128), F32)
     for group in range(8):
         out = jnp.concatenate([out_ref[2 * group], out_ref[2 * group + 1]], axis=0)
@@ -335,6 +371,8 @@
     )
     for n, copy in enumerate(copies):
         copy.wait()
+        if n + 3 < 8:
+            copies[n + 3].start()
         result_ref[n] = lax.dot_general(
             grads,
             store[n * rows : (n + 1) * rows, :],
@@ -345,19 +383,26 @@
 
 def score(flags, out, own, sib, seq, store):
     here = pl.BlockSpec(memory_space=pltpu.VMEM)
+    away = pl.BlockSpec(memory_space=pl.ANY)
     return pl.pallas_call(
         score_kernel,
         in_specs=[
             pl.BlockSpec(memory_space=pltpu.SMEM),
             here,
+            away,
+            away,
             here,
-            here,
-            here,
-            pl.BlockSpec(memory_space=pl.ANY),
+            away,
         ],
         out_specs=here,
         out_shape=jax.ShapeDtypeStruct((8, SEQS, store.shape[0] // 8), F32),
-        scratch_shapes=[pltpu.VMEM(store.shape, BF), pltpu.SemaphoreType.DMA((8,))],
+        scratch_shapes=[
+            pltpu.VMEM(own.shape, F32),
+            pltpu.VMEM(own.shape, F32),
+            pltpu.VMEM(store.shape, BF),
+            pltpu.SemaphoreType.DMA((8,)),
+            pltpu.SemaphoreType.DMA((2,)),
+        ],
         compiler_params=pltpu.CompilerParams(vmem_limit_bytes=48 * 1024 * 1024),
     )(flags, out, own, sib, seq, store)
 
@@ -376,7 +421,7 @@
     quarters = jnp.stack([k, 3 - k]).astype(jnp.int32)
 
     mine, mine_d = rows_of(
-        ((0, (0,), 64, 0, 0), (0, (1,), 64, 1, 0)), quarters, [hidden], [64, 64], 60 << 20
+        ((0, (0,), 64, 0, 0), (0, (1,), 64, 1, 0)), quarters, [hidden], [64, 64], 58 << 20, pltpu.VMEM
     )
     near_a = move(mine, along_x)
     near_b = move(mine, along_x_crossed)
@@ -390,7 +435,7 @@
     near_z = move(near, along_z)
 
     rest = (out_head, head_sib, out_proj, proj_sib, in_proj)
-    first = flash([hidden], *rest)
+    first = flash([hidden], *rest, stream=True)
     first, far_k, near_y, near_z = lax.optimization_barrier((first, far_k, near_y, near_z))
     last_y, last_z = rows_of(
         ((0, 0, 64, 0, 0), (2, 64, 32, 0, 64), (0, 0, 64, 1, 0), (1, 96, 32, 1, 64)),

time: 157 us -> 125 us (0.80)
  Pallas kernels: 74.5 us -> 46.1 us
  local copies, waits for them, and re-layouts: 11.4 us -> 7.94 us
    pallas_call x3, Pallas kernels: 34.9 us -> 4.25 us  [rows_of(): pl.pallas_call(functools.partial(rows_kernel, plan, len(sources)), in_spe...]
    unnamed x28, local copies, waits for them, and re-layouts: 9.84 us -> 6.39 us
    pallas_call x3, Pallas kernels: 27.2 us -> 30.2 us  [flash(): pl.pallas_call(functools.partial(flash_kernel, sizes, stream), in_specs=[...]
  transfers between devices with their start and end apart: 14 -> 14, of which waited for: 4 -> 4; matrix products, arithmetic and copies ran while one was open for 2% -> 2% of each run, Pallas kernels for 37% -> 24%
where the time goes in v4:
time: 125 us; the launch traced here: 124 us
  Pallas kernels  46.1 us (37%)
  waiting for transfers between devices  31.7 us (25%)
  starting transfers between devices  27.1 us (22%)
  blocking collectives  9.5 us (8%)
  local copies, waits for them, and re-layouts  7.94 us (6%)
  other arithmetic  1.38 us (1%)
    pallas_call x3, Pallas kernels, flash(): pl.pallas_call(functools.partial(flash_kernel, sizes, stream), in_specs=[...  30.2 us
    ppermute x12, starting transfers between devices, move(): return lax.ppermute(value, ALL, pairs)  17 us
    all_to_all x1, waiting for transfers between devices, on_device(): got = lax.all_to_all(send, ALL, 0, 0, tiled=True)  15.3 us
    ppermute x12, waiting for transfers between devices, move(): return lax.ppermute(value, ALL, pairs)  9.96 us
    all_to_all x1, blocking collectives, on_device(): lax.all_to_all(partial, ('x', 'c'), 0, 0, tiled=True)  9.5 us
    pallas_call x1, Pallas kernels, score(): pl.pallas_call(score_kernel, in_specs=[pl.BlockSpec(memory_space=pltpu.SM...  7.19 us
    all_to_all x1, starting transfers between devices, on_device(): got = lax.all_to_all(send, ALL, 0, 0, tiled=True)  6.57 us
    all_to_all x1, waiting for transfers between devices, on_device(): out = lax.all_to_all(merge(got), ('y', 'z'), 0, 0, tiled=True)  6.43 us
  transfers between devices with their start and end apart: 14, of which 4 were waited for; matrix products, arithmetic and copies ran while one was open for 2% of the time, Pallas kernels for 24%

profile of v4, /device:TPU:1, one launch (start us, length us, event | category | flops | bytes accessed | tf_op | source)
XLA Modules:
  0.0 124.0 jit_solution(10565764082605597739)
XLA Ops:
  0.0 1.4 %collective-permute-start.1 = (bf16[1024,4096]{1,0:T(8,128)(2,1)}, bf16[1024,4096]{1,0:T(8,128)(2,1)}, u32[]{:S(2)}, u32[]{:S(2)}) collective-permute-start(bf16[1024,4096]{1,0:T(8,128)(2,1)} %refs_3_.3), channel_id=1, source_target_pairs={{0,1},{1,0},{2,3},{3,2},{4,5},{5,4},{6,7},{7,6},{8,9},{9,8},{10,11... | collective-permute-start | bytes 25165832 | tf_op jit(solution)/shard_map/ppermute | solution.py:31
  2.0 2.9 %shard_map.73 = (bf16[64,4096]{1,0:T(8,128)(2,1)}, bf16[64,4096]{1,0:T(8,128)(2,1)}) custom-call(s32[2]{0:T(128)} %pad_add_fusion.refs_0_, bf16[256,4096]{1,0:T(8,128)(2,1)} %refs_0_.1), custom_call_target="tpu_custom_call" | custom-call | bytes 2097152 | tf_op jit(solution)/shard_map/pallas_call | solution.py:77
  4.9 2.6 %collective-permute-start = (bf16[64,4096]{1,0:T(8,128)(2,1)}, bf16[64,4096]{1,0:T(8,128)(2,1)S(1)}, u32[]{:S(2)}, u32[]{:S(2)}) collective-permute-start(bf16[64,4096]{1,0:T(8,128)(2,1)} %get-tuple-element.30), channel_id=1, source_target_pairs={{0,2},{1,7},{2,4},{3,1},{4,6},{5,3},{6,0},{7,5},{8,10},{9,15},{10,... | collective-permute-start | bytes 1572872 | tf_op jit(solution)/shard_map/ppermute | solution.py:31
  9.2 9.3 %collective-permute-done.refs_1_ = bf16[64,4096]{1,0:T(8,128)(2,1)S(1)} collective-permute-done((bf16[64,4096]{1,0:T(8,128)(2,1)}, bf16[64,4096]{1,0:T(8,128)(2,1)S(1)}, u32[]{:S(2)}, u32[]{:S(2)}) %collective-permute-start) | collective-permute-done | bytes 524320 | tf_op jit(solution)/shard_map/ppermute | solution.py:31
  20.4 2.9 %collective-permute-start.5 = (bf16[128,4096]{1,0:T(8,128)(2,1)S(1)}, bf16[128,4096]{1,0:T(8,128)(2,1)S(1)}, u32[]{:S(2)}, u32[]{:S(2)}) collective-permute-start(bf16[128,4096]{1,0:T(8,128)(2,1)S(1)} %shard_map.75.refs_0_), channel_id=1, source_target_pairs={{0,32},{1,97},{2,34},{3,99},{4,36},{5,101},{6,38},{7,103},{8,40},{... | collective-permute-start | bytes 3145736 | tf_op jit(solution)/shard_map/ppermute | solution.py:31
  23.3 3.8 %collective-permute-start.6 = (bf16[128,4096]{1,0:T(8,128)(2,1)S(1)}, bf16[128,4096]{1,0:T(8,128)(2,1)S(1)}, u32[]{:S(2)}, u32[]{:S(2)}) collective-permute-start(bf16[128,4096]{1,0:T(8,128)(2,1)S(1)} %shard_map.75.refs_0_), channel_id=1, source_target_pairs={{0,8},{1,25},{2,10},{3,27},{4,12},{5,29},{6,14},{7,31},{8,16},{9,1... | collective-permute-start | bytes 3145736 | tf_op jit(solution)/shard_map/ppermute | solution.py:31
  27.7 3.4 %collective-permute-start.3 = (bf16[64,4096]{1,0:T(8,128)(2,1)}, bf16[64,4096]{1,0:T(8,128)(2,1)S(1)}, u32[]{:S(2)}, u32[]{:S(2)}) collective-permute-start(bf16[64,4096]{1,0:T(8,128)(2,1)} %copy-done.6), channel_id=1, source_target_pairs={{0,2},{1,7},{2,4},{3,1},{4,6},{5,3},{6,0},{7,5},{8,10},{9,15},{10,... | collective-permute-start | bytes 1572872 | tf_op jit(solution)/shard_map/ppermute | solution.py:31
  31.2 0.9 copy-done.3
  32.2 1.3 %shard_map.79.refs_9_ = f32[128,1024]{1,0:T(8,128)S(1)} custom-call(s32[2]{0:T(128)S(1)} %pad_add_fusion.1.where, s32[1,1024]{1,0:T(1,128)S(1)} %reshape.44.targets_ref, bf16[1024,128]{1,0:T(8,128)(2,1)S(1)} %copy-done.3, bf16[1024,128]{1,0:T(8,128)(2,1)S(1)} %collective-permute-done.2.refs_4_.refs_8_.refs_6_.sib_ref), custom_call_target="tpu_custom_call" | custom-call | flops 536870912 | bytes 1048576 | tf_op jit(solution)/shard_map/pallas_call | solution.py:219
  33.5 1.6 %copy-done = bf16[256,4096]{1,0:T(8,128)(2,1)S(1)} copy-done((bf16[256,4096]{1,0:T(8,128)(2,1)S(1)}, bf16[256,4096]{1,0:T(8,128)(2,1)}, u32[]{:S(2)}) %copy-start) | copy-done | bytes 2097176
  35.1 1.2 copy-done.1
  37.2 10.2 %shard_map.74 = (f32[256,128]{1,0:T(8,128)S(1)}, f32[256,128]{1,0:T(8,128)S(1)}, f32[256,128]{1,0:T(8,128)S(1)}) custom-call(bf16[256,4096]{1,0:T(8,128)(2,1)S(1)} %copy-done, bf16[1024,4096]{1,0:T(8,128)(2,1)} %refs_3_.3, bf16[1024,4096]{1,0:T(8,128)(2,1)} %collective-permute-done.1.refs_2_.refs_6_.refs_4_, bf16[1024,128]{1,0:T(8,128)(2,1)S(1)} %copy-done.4, ...), custom_call_target="tpu_custom_call" | custom-call | flops 4294967296 | bytes 2097152 | tf_op jit(solution)/shard_map/pallas_call | solution.py:181
  49.0 12.7 %shard_map.76 = (f32[512,128]{1,0:T(8,128)S(1)}, f32[512,128]{1,0:T(8,128)S(1)}, f32[512,128]{1,0:T(8,128)S(1)}) custom-call(bf16[128,4096]{1,0:T(8,128)(2,1)S(1)} %shard_map.75.refs_0_, bf16[128,4096]{1,0:T(8,128)(2,1)S(1)} %collective-permute-done.5.refs_1_.refs_2_, bf16[128,4096]{1,0:T(8,128)(2,1)S(1)} %collective-permute-done.6.refs_2_.refs_3_, ...), custom_call_target="tpu_custom_call" | custom-call | flops 8589934592 | bytes 4194304 | tf_op jit(solution)/shard_map/pallas_call | solution.py:181
  61.7 7.3 %shard_map.78 = (f32[256,128]{1,0:T(8,128)S(1)}, f32[256,128]{1,0:T(8,128)S(1)}, f32[256,128]{1,0:T(8,128)S(1)}) custom-call(bf16[96,4096]{1,0:T(8,128)(2,1)S(1)} %collective-permute-done.8.refs_0_, bf16[96,4096]{1,0:T(8,128)(2,1)S(1)} %collective-permute-done.9.refs_1_, bf16[64,4096]{1,0:T(8,128)(2,1)S(1)} %collective-permute-done.10.refs_2_, ...), custom_call_target="tpu_custom_call" | custom-call | flops 4294967296 | bytes 2097152 | tf_op jit(solution)/shard_map/pallas_call | solution.py:181
  69.0 1.8 %shard_map.80 = (bf16[128,24,128]{2,1,0:T(8,128)(2,1)}, f32[8,4,32,128]{3,2,1,0:T(8,128)S(1)}) custom-call(s32[5]{0:T(128)S(1)} %stack.45.place, f32[256,128]{1,0:T(8,128)S(1)} %get-tuple-element.36.refs_0_, f32[512,128]{1,0:T(8,128)S(1)} %get-tuple-element.41.refs_1_, f32[256,128]{1,0:T(8,128)S(1)} %get-tuple-element.44.refs_2_, ...), custom_call_target="tpu_custom_call" | custom-call | tf_op jit(solution)/shard_map/pallas_call | solution.py:277
  70.8 6.6 %all-to-all-start = ((bf16[128,24,128]{2,1,0:T(8,128)(2,1)}), bf16[128,24,128]{2,1,0:T(8,128)(2,1)S(1)}, u32[]{:S(2)}, u32[]{:S(2)}) async-start(bf16[128,24,128]{2,1,0:T(8,128)(2,1)} %get-tuple-element.51), calls=%async_computation | async-start | bytes 1572864 | tf_op jit(solution)/shard_map/all_to_all | solution.py:476
  77.4 1.1 collective-permute-start.11
  78.6 15.3 %all-to-all-done.got_ref = bf16[128,24,128]{2,1,0:T(8,128)(2,1)S(1)} async-done(((bf16[128,24,128]{2,1,0:T(8,128)(2,1)}), bf16[128,24,128]{2,1,0:T(8,128)(2,1)S(1)}, u32[]{:S(2)}, u32[]{:S(2)}) %all-to-all-start) | async-done | bytes 786464 | tf_op jit(solution)/shard_map/all_to_all | solution.py:476
  93.9 1.4 %shard_map.81 = f32[16,8,256]{2,1,0:T(8,128)} custom-call(bf16[128,24,128]{2,1,0:T(8,128)(2,1)S(1)} %all-to-all-done.got_ref), custom_call_target="tpu_custom_call" | custom-call | tf_op jit(solution)/shard_map/pallas_call | solution.py:317
  95.4 3.5 %all-to-all-start.1 = ((f32[16,8,256]{2,1,0:T(8,128)}), f32[16,8,256]{2,1,0:T(8,128)S(1)}, u32[]{:S(2)}, u32[]{:S(2)}) async-start(f32[16,8,256]{2,1,0:T(8,128)} %shard_map.81), calls=%async_computation.1 | async-start | bytes 262144 | tf_op jit(solution)/shard_map/all_to_all | solution.py:478
  99.2 6.4 %all-to-all-done.1.out_ref = f32[16,8,256]{2,1,0:T(8,128)S(1)} async-done(((f32[16,8,256]{2,1,0:T(8,128)}), f32[16,8,256]{2,1,0:T(8,128)S(1)}, u32[]{:S(2)}, u32[]{:S(2)}) %all-to-all-start.1) | async-done | bytes 131104 | tf_op jit(solution)/shard_map/all_to_all | solution.py:478
  105.7 1.0 copy-done.8
  106.7 7.2 %shard_map.82 = f32[8,16,256]{2,1,0:T(8,128)S(1)} custom-call(s32[4]{0:T(128)S(1)} %get-tuple-element.58.flags, f32[16,8,256]{2,1,0:T(8,128)S(1)} %all-to-all-done.1.out_ref, f32[8,4,32,128]{3,2,1,0:T(8,128)S(1)} %copy-done.8, f32[8,4,32,128]{3,2,1,0:T(8,128)S(1)} %collective-permute-done.11.sib_hbm, s32[8,256]{1,0:T(8,128)S(1)} %reshape.46.seq_ref, ...), custom_call_target="tpu_custom_call" | custom-call | tf_op jit(solution)/shard_map/pallas_call | solution.py:387
  113.9 9.5 %all_to_all.15 = f32[8,16,256]{2,1,0:T(8,128)S(1)} all-to-all(f32[8,16,256]{2,1,0:T(8,128)S(1)} %shard_map.82), channel_id=1, replica_groups=mesh['y'=4,'z'=4,'x'=4,'c'=2] {'x','c'}, dimensions={0} | all-to-all | bytes 262144 | tf_op jit(solution)/shard_map/all_to_all | solution.py:480
  (67 shorter events, 8.3 us)
Async XLA Ops:
  0.0 18.5 %collective-permute-start.1 = (bf16[1024,4096]{1,0:T(8,128)(2,1)}, bf16[1024,4096]{1,0:T(8,128)(2,1)}, u32[]{:S(2)}, u32[]{:S(2)}) collective-permute-start(bf16[1024,4096]{1,0:T(8,128)(2,1)} %refs_3_.3), channel_id=1, source_target_pairs={{0,1},{1,0},{2,3},{3,2},{4,5},{5,4},{6,7},{7,6},{8,9},{9,8},{10,11... | collective-permute-start | bytes 25165832 | tf_op jit(solution)/shard_map/ppermute | solution.py:31
  4.9 13.5 %collective-permute-start = (bf16[64,4096]{1,0:T(8,128)(2,1)}, bf16[64,4096]{1,0:T(8,128)(2,1)S(1)}, u32[]{:S(2)}, u32[]{:S(2)}) collective-permute-start(bf16[64,4096]{1,0:T(8,128)(2,1)} %get-tuple-element.30), channel_id=1, source_target_pairs={{0,2},{1,7},{2,4},{3,1},{4,6},{5,3},{6,0},{7,5},{8,10},{9,15},{10,... | collective-permute-start | bytes 1572872 | tf_op jit(solution)/shard_map/ppermute | solution.py:31
  7.6 11.6 %collective-permute-start.4 = (bf16[64,4096]{1,0:T(8,128)(2,1)}, bf16[64,4096]{1,0:T(8,128)(2,1)S(1)}, u32[]{:S(2)}, u32[]{:S(2)}) collective-permute-start(bf16[64,4096]{1,0:T(8,128)(2,1)} %get-tuple-element.30), channel_id=1, source_target_pairs={{0,7},{1,2},{2,1},{3,4},{4,3},{5,6},{6,5},{7,0},{8,15},{9,10},{10,... | collective-permute-start | bytes 1572872 | tf_op jit(solution)/shard_map/ppermute | solution.py:31
  7.7 23.5 %collective-permute-start.2 = (bf16[1024,128]{1,0:T(8,128)(2,1)}, bf16[1024,128]{1,0:T(8,128)(2,1)S(1)}, u32[]{:S(2)}, u32[]{:S(2)}) collective-permute-start(bf16[1024,128]{1,0:T(8,128)(2,1)} %own_ref.1), channel_id=1, source_target_pairs={{0,1},{1,0},{2,3},{3,2},{4,5},{5,4},{6,7},{7,6},{8,9},{9,8},{10,11... | collective-permute-start | bytes 786440 | tf_op jit(solution)/shard_map/ppermute | solution.py:31
  18.5 1.9 %copy-start.6 = (bf16[64,4096]{1,0:T(8,128)(2,1)}, bf16[64,4096]{1,0:T(8,128)(2,1)S(1)}, u32[]{:S(2)}) copy-start(bf16[64,4096]{1,0:T(8,128)(2,1)S(1)} %collective-permute-done.refs_1_) | copy-start | bytes 1572868
  20.4 27.2 %collective-permute-start.5 = (bf16[128,4096]{1,0:T(8,128)(2,1)S(1)}, bf16[128,4096]{1,0:T(8,128)(2,1)S(1)}, u32[]{:S(2)}, u32[]{:S(2)}) collective-permute-start(bf16[128,4096]{1,0:T(8,128)(2,1)S(1)} %shard_map.75.refs_0_), channel_id=1, source_target_pairs={{0,32},{1,97},{2,34},{3,99},{4,36},{5,101},{6,38},{7,103},{8,40},{... | collective-permute-start | bytes 3145736 | tf_op jit(solution)/shard_map/ppermute | solution.py:31
  23.3 24.3 %collective-permute-start.6 = (bf16[128,4096]{1,0:T(8,128)(2,1)S(1)}, bf16[128,4096]{1,0:T(8,128)(2,1)S(1)}, u32[]{:S(2)}, u32[]{:S(2)}) collective-permute-start(bf16[128,4096]{1,0:T(8,128)(2,1)S(1)} %shard_map.75.refs_0_), channel_id=1, source_target_pairs={{0,8},{1,25},{2,10},{3,27},{4,12},{5,29},{6,14},{7,31},{8,16},{9,1... | collective-permute-start | bytes 3145736 | tf_op jit(solution)/shard_map/ppermute | solution.py:31
  27.7 19.9 %collective-permute-start.3 = (bf16[64,4096]{1,0:T(8,128)(2,1)}, bf16[64,4096]{1,0:T(8,128)(2,1)S(1)}, u32[]{:S(2)}, u32[]{:S(2)}) collective-permute-start(bf16[64,4096]{1,0:T(8,128)(2,1)} %copy-done.6), channel_id=1, source_target_pairs={{0,2},{1,7},{2,4},{3,1},{4,6},{5,3},{6,0},{7,5},{8,10},{9,15},{10,... | collective-permute-start | bytes 1572872 | tf_op jit(solution)/shard_map/ppermute | solution.py:31
  31.1 16.4 %collective-permute-start.7 = (bf16[64,4096]{1,0:T(8,128)(2,1)}, bf16[64,4096]{1,0:T(8,128)(2,1)S(1)}, u32[]{:S(2)}, u32[]{:S(2)}) collective-permute-start(bf16[64,4096]{1,0:T(8,128)(2,1)} %get-tuple-element.40), channel_id=1, source_target_pairs={{0,2},{1,7},{2,4},{3,1},{4,6},{5,3},{6,0},{7,5},{8,10},{9,15},{10,... | collective-permute-start | bytes 1572872 | tf_op jit(solution)/shard_map/ppermute | solution.py:31
  32.2 16.8 %slice-start = ((s8[8388608]{0:T(1024)(128)(4,1)}), s8[4194304]{0:T(1024)(128)(4,1)S(1)}, s32[]{:S(2)}) async-start(s8[8388608]{0:T(1024)(128)(4,1)} %bitcast.13), calls=%async_computation.3 | async-start | bytes 8388608
  33.5 1.6 %copy-start = (bf16[256,4096]{1,0:T(8,128)(2,1)S(1)}, bf16[256,4096]{1,0:T(8,128)(2,1)}, u32[]{:S(2)}) copy-start(bf16[256,4096]{1,0:T(8,128)(2,1)} %refs_0_.1) | copy-start | bytes 6291460
  35.1 1.2 copy-start.1
  37.2 10.4 %copy-start.10 = (s32[2]{0:T(128)S(1)}, s32[2]{0:T(128)}, u32[]{:S(2)}) copy-start(s32[2]{0:T(128)} %pad_add_fusion.refs_0_) | copy-start | bytes 28
  37.2 11.7 %slice-start.1 = ((s8[8388608]{0:T(1024)(128)(4,1)}), s8[4194304]{0:T(1024)(128)(4,1)S(1)}, s32[]{:S(2)}) async-start(s8[8388608]{0:T(1024)(128)(4,1)} %bitcast.13), calls=%async_computation.4 | async-start | bytes 8388608
  37.2 11.7 %copy-start.2 = (bf16[4096,128]{1,0:T(8,128)(2,1)S(1)}, bf16[4096,128]{1,0:T(8,128)(2,1)}, u32[]{:S(2)}) copy-start(bf16[4096,128]{1,0:T(8,128)(2,1)} %refs_7_.3) | copy-start | bytes 3145732
  37.2 11.7 %copy-start.5 = (bf16[1024,128]{1,0:T(8,128)(2,1)S(1)}, bf16[1024,128]{1,0:T(8,128)(2,1)}, u32[]{:S(2)}) copy-start(bf16[1024,128]{1,0:T(8,128)(2,1)} %own_ref.1) | copy-start | bytes 786436
  47.5 14.2 %collective-permute-start.10 = (bf16[64,4096]{1,0:T(8,128)(2,1)S(1)}, bf16[64,4096]{1,0:T(8,128)(2,1)S(1)}, u32[]{:S(2)}, u32[]{:S(2)}) collective-permute-start(bf16[64,4096]{1,0:T(8,128)(2,1)S(1)} %collective-permute-done.7.refs_4_), channel_id=1, source_target_pairs={{0,2},{1,7},{2,4},{3,1},{4,6},{5,3},{6,0},{7,5},{8,10},{9,15},{10,... | collective-permute-start | bytes 1572872 | tf_op jit(solution)/shard_map/ppermute | solution.py:31
  48.3 13.4 %collective-permute-start.8 = (bf16[96,4096]{1,0:T(8,128)(2,1)S(1)}, bf16[96,4096]{1,0:T(8,128)(2,1)S(1)}, u32[]{:S(2)}, u32[]{:S(2)}) collective-permute-start(bf16[96,4096]{1,0:T(8,128)(2,1)S(1)} %get-tuple-element.42), channel_id=1, source_target_pairs={{0,32},{1,97},{2,34},{3,99},{4,36},{5,101},{6,38},{7,103},{8,40},{... | collective-permute-start | bytes 2359304 | tf_op jit(solution)/shard_map/ppermute | solution.py:31
  48.8 12.8 %collective-permute-start.9 = (bf16[96,4096]{1,0:T(8,128)(2,1)S(1)}, bf16[96,4096]{1,0:T(8,128)(2,1)S(1)}, u32[]{:S(2)}, u32[]{:S(2)}) collective-permute-start(bf16[96,4096]{1,0:T(8,128)(2,1)S(1)} %get-tuple-element.43), channel_id=1, source_target_pairs={{0,8},{1,25},{2,10},{3,27},{4,12},{5,29},{6,14},{7,31},{8,16},{9,1... | collective-permute-start | bytes 2359304 | tf_op jit(solution)/shard_map/ppermute | solution.py:31
  61.6 16.9 %copy-start.11 = (s32[2048]{0:T(1024)S(1)}, s32[2048]{0:T(1024)}, u32[]{:S(2)}) copy-start(s32[2048]{0:T(1024)} %param.12) | copy-start | bytes 24580
  70.8 34.9 %copy-start.7 = (f32[8,4,32,128]{3,2,1,0:T(8,128)}, f32[8,4,32,128]{3,2,1,0:T(8,128)S(1)}, u32[]{:S(2)}) copy-start(f32[8,4,32,128]{3,2,1,0:T(8,128)S(1)} %get-tuple-element.52.own_hbm) | copy-start | bytes 1572868
  70.8 23.1 %all-to-all-start = ((bf16[128,24,128]{2,1,0:T(8,128)(2,1)}), bf16[128,24,128]{2,1,0:T(8,128)(2,1)S(1)}, u32[]{:S(2)}, u32[]{:S(2)}) async-start(bf16[128,24,128]{2,1,0:T(8,128)(2,1)} %get-tuple-element.51), calls=%async_computation | async-start | bytes 1572864 | tf_op jit(solution)/shard_map/all_to_all | solution.py:476
  77.4 21.9 %collective-permute-start.11 = (f32[8,4,32,128]{3,2,1,0:T(8,128)S(1)}, f32[8,4,32,128]{3,2,1,0:T(8,128)S(1)}, u32[]{:S(2)}, u32[]{:S(2)}) collective-permute-start(f32[8,4,32,128]{3,2,1,0:T(8,128)S(1)} %get-tuple-element.52.own_hbm), channel_id=1, source_target_pairs={{0,1},{1,0},{2,3},{3,2},{4,5},{5,4},{6,7},{7,6},{8,9},{9,8},{10,11... | collective-permute-start | bytes 1572872 | tf_op jit(solution)/shard_map/ppermute | solution.py:31
  95.4 10.3 %all-to-all-start.1 = ((f32[16,8,256]{2,1,0:T(8,128)}), f32[16,8,256]{2,1,0:T(8,128)S(1)}, u32[]{:S(2)}, u32[]{:S(2)}) async-start(f32[16,8,256]{2,1,0:T(8,128)} %shard_map.81), calls=%async_computation.1 | async-start | bytes 262144 | tf_op jit(solution)/shard_map/all_to_all | solution.py:478
  (4 other events, 3.6 us)
